TPU v7x, 128 devices: a whole 4x4x4 slice. The times are simulated.
128 devices in a mesh: ctx: 16 (over z, x_lo, core), tp: 8 (over y, x_hi).
Axes of the slice: x: 4 (x_hi: 2, x_lo: 2; x = x_hi * 2 + x_lo), y: 4, z: 4, core: 2. Of those that a mesh axis runs over, the one named last changes fastest.
Arguments:
- tokens: bfloat16 [64, 256, 2048], P('ctx'), may hold values from -6 to 6
- block_lists: int32 [16, 4], replicated, may hold values from 0 to 15, as said below
- gain_attn: float32 [2048], replicated, may hold values from 0.5 to 1.5
- w_qkv: bfloat16 [2048, 3, 2048], P(None, None, 'tp'), may hold values from -3 to 3
- w_out: bfloat16 [2048, 2048], P('tp'), may hold values from -0.1875 to 0.1875
- gain_mlp: float32 [2048], replicated, may hold values from 0.5 to 1.5
- w_up: bfloat16 [2048, 8192], P(None, 'tp'), may hold values from -0.125 to 0.125
- w_down: bfloat16 [8192, 2048], P('tp'), may hold values from -0.09375 to 0.09375
Outputs:
- layer_out: bfloat16 [64, 256, 2048], P('ctx', None, 'tp')
Inputs may be any that keep to these rules, and one draw needn't show every extreme that they name: `block_lists`: row i starts with i itself, then i - 1 (0 for row 0); the remaining entries step back from i by a stride of 2 to 4 blocks drawn for each row, one and two strides, clamped at 0; every entry lies between 0 and i.
All inputs are finite; a program needn't handle non-finite values.
Results may differ from a plain program's by a relative error of at most 0.015.
Values may be sent and summed in bfloat16 or wider, within the bound.
A program may use at most 128 MiB of HBM per device.

v0:
```python
import jax
import jax.numpy as jnp
from jax import lax
from jax.sharding import PartitionSpec as P

HD = 128


negative_fill = -1e30


def layer_norm(values, gain):
    centre = jnp.mean(values, axis=-1, keepdims=True)
    centred = values - centre
    variance = jnp.mean(centred * centred, axis=-1, keepdims=True)
    return centred * lax.rsqrt(variance + 1e-05) * gain


def column_update(running, queries, key_piece, value_piece, allowed):
    running_max, weight_sum, weighted = running
    scores = jnp.einsum(
        "rchd,schd->rchs", queries, key_piece, preferred_element_type=jnp.float32
    ) * HD ** (-0.5)
    masked = allowed[:, None, None, :]
    scores = jnp.where(masked, scores, negative_fill)
    new_max = jnp.maximum(running_max, jnp.max(scores, axis=-1))
    weights = jnp.where(masked, jnp.exp(scores - new_max[..., None]), 0.0)
    shrink = jnp.exp(running_max - new_max)
    weight_sum = weight_sum * shrink + jnp.sum(weights, axis=-1)
    weighted = weighted * shrink[..., None] + jnp.einsum(
        "rchs,schd->rchd", weights, value_piece.astype(jnp.float32), precision=lax.Precision.HIGHEST
    )
    return (new_max, weight_sum, weighted)


def on_device(tokens, block_lists, gain_attn, w_qkv, w_out, gain_mlp, w_up, w_down):
    rows_dev, slab_cols, width = tokens.shape
    heads_here = w_qkv.shape[2] // HD
    ctx_index = lax.axis_index("ctx")
    tp_index = lax.axis_index("tp")
    blocks_all = block_lists.shape[0]
    listed = jnp.any(block_lists[:, :, None] == jnp.arange(blocks_all)[None, None, :], axis=1)
    flat_tokens = tokens.reshape(rows_dev * slab_cols, width).astype(jnp.float32)
    normed = layer_norm(flat_tokens, gain_attn).astype(jnp.bfloat16)
    projected = jnp.dot(
        normed, w_qkv.reshape(width, 3 * heads_here * HD), preferred_element_type=jnp.float32
    )
    projected = projected.astype(jnp.bfloat16).reshape(rows_dev, slab_cols, 3, heads_here, HD)
    queries = projected[:, :, 0]
    key_heads = projected[:, :, 1]
    value_heads = projected[:, :, 2]
    col_ids = jnp.arange(slab_cols)
    causal = col_ids[None, :] <= col_ids[:, None]
    row_scores = jnp.einsum(
        "rchd,rehd->rhce", queries, key_heads, preferred_element_type=jnp.float32
    ) * HD ** (-0.5)
    row_scores = jnp.where(causal, row_scores, negative_fill)
    row_max = jnp.max(row_scores, axis=-1)
    row_weights = jnp.where(causal, jnp.exp(row_scores - row_max[..., None]), 0.0)
    row_sum = jnp.transpose(jnp.sum(row_weights, axis=-1), (0, 2, 1))
    row_weighted = jnp.einsum(
        "rhce,rehd->rchd",
        row_weights,
        value_heads.astype(jnp.float32),
        precision=lax.Precision.HIGHEST,
    )
    row_max = jnp.transpose(row_max, (0, 2, 1))
    query_rows = ctx_index * rows_dev + jnp.arange(rows_dev)
    query_listed = listed[query_rows // rows_dev]
    key_piece = lax.all_gather(key_heads, "ctx", axis=0, tiled=True)
    value_piece = lax.all_gather(value_heads, "ctx", axis=0, tiled=True)
    key_rows = jnp.arange(key_piece.shape[0])
    allowed = query_listed[:, key_rows // rows_dev] & (key_rows[None, :] < query_rows[:, None])
    joint_max, weight_sum, weighted = column_update(
        (row_max, row_sum, row_weighted), queries, key_piece, value_piece, allowed
    )
    attended = (
        (weighted / weight_sum[..., None])
        .astype(jnp.bfloat16)
        .reshape(rows_dev * slab_cols, heads_here * HD)
    )
    head_terms = jnp.dot(attended, w_out, preferred_element_type=jnp.float32)
    share_cols = width // lax.axis_size("tp")
    summed = lax.psum(head_terms.astype(jnp.bfloat16), "tp").astype(jnp.float32)
    residual = flat_tokens + summed
    normed_mlp = layer_norm(residual, gain_mlp).astype(jnp.bfloat16)
    residual_share = lax.dynamic_slice_in_dim(residual, tp_index * share_cols, share_cols, 1)
    activated = jax.nn.gelu(jnp.dot(normed_mlp, w_up, preferred_element_type=jnp.float32)).astype(
        jnp.bfloat16
    )
    down_terms = jnp.dot(activated, w_down, preferred_element_type=jnp.float32)
    mlp_share = lax.psum_scatter(
        down_terms.astype(jnp.bfloat16), "tp", scatter_dimension=1, tiled=True
    ).astype(jnp.float32)
    return (
        (residual_share + mlp_share).astype(jnp.bfloat16).reshape(rows_dev, slab_cols, share_cols)
    )


def solution(mesh):
    return jax.shard_map(
        on_device,
        mesh=mesh,
        in_specs=(
            P("ctx", None, None),
            P(),
            P(),
            P(None, None, "tp"),
            P("tp", None),
            P(),
            P(None, "tp"),
            P("tp", None),
        ),
        out_specs=P("ctx", None, "tp"),
        check_vma=False,
    )
```

profile of v0, /device:TPU:0, one launch (start us, length us, event | category | flops | bytes accessed | tf_op | source)
XLA Modules:
  0.0 472.0 jit_solution(12313367123321986376)
XLA Ops:
  6.5 3.0 convert_reduce_fusion
  9.5 0.6 copy-done.2
  10.1 1.2 multiply_reduce_fusion.1
  11.3 4.7 copy.88
  16.0 3.2 multiply_convert_fusion.1
  19.2 4.6 convolution_convert_fusion.2
  23.9 3.3 reshape.200
  27.2 0.0 copy-start.9
  27.2 1.9 fusion.72
  29.1 0.8 copy-done.6
  29.9 0.9 copy.157
  30.8 0.0 all-gather.5.cloned.1.call-update
  30.8 0.0 all-gather.7.cloned.1.call-start
  30.8 0.9 copy.101
  31.7 0.0 all-gather.7.cloned.1.call-update
  31.7 0.2 all-reduce.2.cloned.1.call-start
  32.0 1.1 copy.110
  33.1 0.1 fusion.56
  33.2 0.6 gather_fusion
  33.7 0.1 copy.94
  33.9 0.6 gather_fusion.1
  34.5 0.1 copy.95
  34.6 0.9 copy.156
  35.5 0.1 fusion.59
  35.6 1.7 fusion.23
  37.3 0.5 fusion.24
  37.8 47.8 %all-gather.5.cloned.1.call-done = bf16[64,256,1,2,128]{4,1,3,2,0:T(8,128)(2,1)} async-done(((bf16[4,256,1,2,128]{4,1,3,2,0:T(8,128)(2,1)}), bf16[64,256,1,2,128]{4,1,3,2,0:T(8,128)(2,1)}) %all-gather.5.cloned.1.call-update) | async-done | bytes 8388624 | tf_op jit(solution)/shard_map/all_gather | solution.py:70
  85.5 13.2 %fusion.73 = (f32[4,256,2]{0,2,1:T(2,128)S(1)}, f32[4,256,2,64]{3,0,2,1:T(4,128)}) fusion(bf16[4,256,2,128]{3,1,2,0:T(8,128)(2,1)} %bitcast.88, bf16[64,256,1,2,128]{4,1,3,2,0:T(8,128)(2,1)} %all-gather.5.cloned.1.call-done, pred[4,64]{1,0:T(4,128)(4,1)S(1)} %fusion.59), kind=kOutput, calls=%fused_computation.106 | convolution fusion | flops 33945600 | bytes 9445632 | tf_op jit(solution)/shard_map/rchd,schd->rchs/dot_general | solution.py:21
  98.8 0.1 copy.99
  98.9 0.2 copy.103
  99.1 3.2 fusion.45
  102.3 1.1 copy.106
  103.4 37.0 %all-gather.7.cloned.1.call-done = bf16[64,256,1,2,128]{4,1,3,2,0:T(8,128)(2,1)} async-done(((bf16[4,256,1,2,128]{4,1,3,2,0:T(8,128)(2,1)}), bf16[64,256,1,2,128]{4,1,3,2,0:T(8,128)(2,1)}) %all-gather.7.cloned.1.call-update) | async-done | bytes 8388624 | tf_op jit(solution)/shard_map/all_gather | solution.py:71
  140.4 16.0 %fusion = f32[256,2,128,4]{2,3,1,0:T(4,128)} fusion(bf16[64,256,1,2,128]{4,1,3,2,0:T(8,128)(2,1)} %all-gather.7.cloned.1.call-done, f32[4,256,2,64]{3,0,2,1:T(4,128)} %get-tuple-element.13, f32[4,256,2]{0,2,1:T(2,128)S(1)} %copy.103, pred[4,64]{1,0:T(4,128)(4,1)S(1)} %fusion.59), kind=kOutput, calls=%fused_computation.2 | convolution fusion | flops 201588736 | bytes 9969920 | tf_op jit(solution)/shard_map/rchs,schd->rchd/dot_general | solution.py:30
  156.4 2.6 copy.104
  159.0 3.6 fusion.36
  162.6 1.3 copy.108
  163.9 3.2 convolution_convert_fusion
  167.2 0.0 all-reduce.2.cloned.1.call-update
  167.2 0.0 reduce-scatter.2.cloned.1.call-start
  167.2 185.9 %all-reduce.2.cloned.1.call-done = bf16[1024,2048]{1,0:T(8,128)(2,1)} async-done(((bf16[1024,2048]{1,0:T(8,128)(2,1)}), bf16[1024,2048]{1,0:T(8,128)(2,1)}) %all-reduce.2.cloned.1.call-update) | async-done | bytes 4194320 | tf_op jit(solution)/shard_map/psum | solution.py:84
  353.1 4.8 %fusion.70 = f32[1024]{0:T(1024)S(1)} fusion(bf16[1024,2048]{1,0:T(8,128)(2,1)} %all-reduce.2.cloned.1.call-done, bf16[4,256,2048]{2,1,0:T(8,128)(2,1)} %param.8), kind=kLoop, calls=%fused_computation.104 | loop fusion | flops 8387584 | bytes 8392704 | tf_op jit(solution)/shard_map/reduce_sum | solution.py:13
  357.9 1.1 copy-done.4
  359.1 4.2 multiply_reduce_fusion
  363.3 16.2 %convolution_convert_fusion.1 = bf16[1024,2048]{1,0:T(8,128)(2,1)} fusion(bf16[1024,2048]{1,0:T(8,128)(2,1)} %param.15, bf16[2048,1024]{1,0:T(8,128)(2,1)} %param.14, f32[1024,2048]{1,0:T(8,128)} %get-tuple-element.8, f32[2048]{0:T(1024)S(1)} %copy-done.10, f32[1024]{0:T(1024)S(1)} %add_rsqrt_fusion, f32[1024]{0:T(1024)S(1)} %broadcast_multiply_fusion), kind=kOutput, calls=%fused_computation.28 | convolution fusion | flops 8609857536 | bytes 20987904 | tf_op jit(solution)/shard_map/dot_general | solution.py:91
  379.5 0.0 reduce-scatter.2.cloned.1.call-update
  379.5 83.7 %reduce-scatter.2.cloned.1.call-done = bf16[1024,256]{1,0:T(8,128)(2,1)} async-done(((bf16[1024,2048]{1,0:T(8,128)(2,1)}), bf16[1024,256]{1,0:T(8,128)(2,1)}) %reduce-scatter.2.cloned.1.call-update) | async-done | bytes 524304 | tf_op jit(solution)/shard_map/reduce_scatter | solution.py:92
  463.2 2.3 add_convert_fusion
  (33 shorter events, 0.2 us)
Async XLA Ops:
  6.5 157.4 %copy-start = (bf16[256,2048]{1,0:T(8,128)(2,1)S(1)}, bf16[256,2048]{1,0:T(8,128)(2,1)}, u32[]{:S(2)}) copy-start(bf16[256,2048]{1,0:T(8,128)(2,1)} %param.12) | copy-start | bytes 3145732
  6.5 79.0 %all-gather.5.cloned.1.call-start = ((), (), s32[]{:S(2)}) async-start(), calls=%async_computation.3 | async-start | bytes 8912896 | tf_op jit(solution)/shard_map/all_gather | solution.py:70
  6.5 3.5 copy-start.2
  11.3 4.7 %copy-start.8 = (f32[2048]{0:T(1024)S(1)}, f32[2048]{0:T(1024)}, u32[]{:S(2)}) copy-start(f32[2048]{0:T(1024)} %param.10) | copy-start | bytes 24580
  16.0 3.2 copy-start.5
  27.2 5.9 %copy-start.9 = (s32[16,4]{0,1:T(4,128)S(1)}, s32[16,4]{0,1:T(4,128)}, u32[]{:S(2)}) copy-start(s32[16,4]{0,1:T(4,128)} %param.9) | copy-start | bytes 772
  29.1 0.8 copy-start.6
  29.1 5.5 %copy-start.7 = (bf16[4,256,1,2,128]{4,3,2,1,0:T(2,128)(2,1)S(1)}, bf16[4,256,1,2,128]{4,3,2,1,0:T(2,128)(2,1)}, u32[]{:S(2)}) copy-start(bf16[4,256,1,2,128]{4,3,2,1,0:T(2,128)(2,1)} %get-tuple-element.11) | copy-start | bytes 1572868
  30.8 109.6 %all-gather.7.cloned.1.call-start = ((), (), s32[]{:S(2)}) async-start(), calls=%async_computation.4 | async-start | bytes 8912896 | tf_op jit(solution)/shard_map/all_gather | solution.py:71
  31.7 321.4 %all-reduce.2.cloned.1.call-start = ((), (), s32[]{:S(2)}) async-start(), calls=%async_computation.1 | async-start | bytes 8388608 | tf_op jit(solution)/shard_map/psum | solution.py:84
  167.2 296.0 %reduce-scatter.2.cloned.1.call-start = ((), (), s32[]{:S(2)}) async-start(), calls=%async_computation.2 | async-start | bytes 4718592 | tf_op jit(solution)/shard_map/reduce_scatter | solution.py:92
  353.1 4.8 %copy-start.3 = (bf16[4,256,2048]{2,1,0:T(8,128)(2,1)S(1)}, bf16[4,256,2048]{2,1,0:T(8,128)(2,1)}, u32[]{:S(2)}) copy-start(bf16[4,256,2048]{2,1,0:T(8,128)(2,1)} %param.8) | copy-start | bytes 12582916
  353.1 5.9 %copy-start.4 = (bf16[1024,2048]{1,0:T(8,128)(2,1)S(1)}, bf16[1024,2048]{1,0:T(8,128)(2,1)}, u32[]{:S(2)}) copy-start(bf16[1024,2048]{1,0:T(8,128)(2,1)} %all-reduce.2.cloned.1.call-done) | copy-start | bytes 12582916
  359.1 4.2 copy-start.10
  363.3 102.2 %copy-start.1 = (bf16[256,2048]{1,0:T(8,128)(2,1)S(1)}, bf16[256,2048]{1,0:T(8,128)(2,1)}, u32[]{:S(2)}) copy-start(bf16[256,2048]{1,0:T(8,128)(2,1)} %param.12) | copy-start | bytes 3145732
Sparse Core Ops, SparseCore 0:
  30.9 54.6 all-gather.4
  87.3 53.1 all-gather.6
  167.3 185.7 all-reduce.1
  379.6 83.5 reduce-scatter.1
where the time goes:
time: 472 us
  waiting for transfers between devices  354 us (75%)
  matrix products  58.6 us (12%)
  local copies, waits for them, and re-layouts  22.8 us (5%)
  other arithmetic  22.6 us (5%)
  between operations  13.3 us (3%)
    psum x1, waiting for transfers between devices, on_device(): summed = lax.psum(head_terms.astype(jnp.bfloat16), 'tp').astype(jnp.float32)  186 us
    reduce_scatter x1, waiting for transfers between devices, on_device(): lax.psum_scatter(down_terms.astype(jnp.bfloat16), 'tp', scatter_dimension...  83.7 us
    all_gather x1, waiting for transfers between devices, on_device(): key_piece = lax.all_gather(key_heads, 'ctx', axis=0, tiled=True)  47.8 us
    all_gather x1, waiting for transfers between devices, on_device(): value_piece = lax.all_gather(value_heads, 'ctx', axis=0, tiled=True)  37 us
    dot_general x1, matrix products, on_device(): down_terms = jnp.dot(activated, w_down, preferred_element_type=jnp.float32)  16.2 us
    dot_general x1, matrix products, column_update(): jnp.einsum('rchs,schd->rchd', weights, value_piece.astype(jnp.float32), p...  16 us
    dot_general x1, matrix products, column_update(): jnp.einsum('rchd,schd->rchs', queries, key_piece, preferred_element_type=...  13.2 us
    unnamed x26, local copies, waits for them, and re-layouts  10.1 us
  transfers between devices with their start and end apart: 4, of which 4 were waited for; matrix products, arithmetic and copies ran while one was open for 5% of the time, Pallas kernels for 0%

commit v1 on v0

v1 whole, which is shorter than its diff:
```python
import functools

import jax
import jax.numpy as jnp
from jax import lax
from jax.experimental import pallas as pl
from jax.experimental.pallas import tpu as pltpu
from jax.sharding import PartitionSpec as P

HD = 128
MESH = pl.DeviceIdType.MESH
NEG = -1e30
BF = jnp.bfloat16
F32 = jnp.float32


def remote(src, dst, send_sem, recv_sem, device):
    return pltpu.make_async_remote_copy(
        src_ref=src, dst_ref=dst, send_sem=send_sem, recv_sem=recv_sem, device_id=device, device_id_type=MESH
    )


def layer_norm(values, gain):
    centre = jnp.mean(values, axis=-1, keepdims=True)
    centred = values - centre
    variance = jnp.mean(centred * centred, axis=-1, keepdims=True)
    return centred * lax.rsqrt(variance + 1e-05) * gain


def dot(a, b):
    return jnp.dot(a, b, preferred_element_type=F32)


def dot_t(a, b):
    return lax.dot_general(a, b, (((1,), (1,)), ((), ())), preferred_element_type=F32)


def attn_kernel(
    lists, tok_ref, gain_ref, wqkv_ref, wout_ref, att_ref, wfull_ref,
    tok, wqkv, normed, qkv, recv, colout, ret, acc, maxes, sums,
    load_sem, own_sem, send_sem, recv_sem, back_send, back_recv, wo_send, wo_recv, wc_send, wc_recv,
):
    n_ctx, rows, cols, feats = 16, 4, 256, 768
    share = cols // n_ctx
    ctx = lax.axis_index("ctx")
    tp = lax.axis_index("tp")
    core = lax.rem(ctx, 2)
    sibling = ctx + 1 - 2 * core

    loads = [pltpu.make_async_copy(wqkv_ref, wqkv, load_sem.at[4])]
    for r in range(rows):
        loads.append(pltpu.make_async_copy(tok_ref.at[pl.ds(r * cols, cols), :], tok.at[r], load_sem.at[r]))
    loads[1].start()
    loads[0].start()
    for r in range(1, rows):
        loads[r + 1].start()
    own_w = pltpu.make_async_copy(wout_ref, wfull_ref.at[pl.ds(pl.multiple_of(tp * 256, 256), 256), :], own_sem.at[0])
    own_w.start()

    barrier = pltpu.get_barrier_semaphore()
    for k in range(1, n_ctx):
        pl.semaphore_signal(barrier, inc=1, device_id={"ctx": lax.rem(ctx + k, n_ctx)}, device_id_type=MESH)
    for k in range(1, 8):
        pl.semaphore_signal(barrier, inc=1, device_id={"tp": lax.rem(tp + k, 8)}, device_id_type=MESH)
    pl.semaphore_wait(barrier, n_ctx - 1 + 7)

    def half(owner, which):
        return pl.ds(pl.multiple_of(owner * 256 + which * 128, 128), 128)

    gather = []
    for k in range(1, 8):
        gather.append(
            remote(
                wout_ref.at[pl.ds(pl.multiple_of(core * 128, 128), 128), :],
                wfull_ref.at[half(tp, core), :],
                wo_send.at[k - 1], wo_recv.at[k - 1], {"tp": lax.rem(tp + k, 8)},
            )
        )
        gather[-1].start()

    loads[0].wait()

    def row_share(j):
        return pl.ds(pl.multiple_of(j * share, share), share)

    @pl.loop(0, rows)
    def _(r):
        pltpu.make_async_copy(tok_ref.at[pl.ds(0, cols), :], tok.at[r], load_sem.at[r]).wait()

        @pl.loop(0, cols // 64)
        def _(b):
            part = pl.ds(pl.multiple_of(b * 64, 64), 64)
            normed[part, :] = layer_norm(tok[r, part, :].astype(F32), gain_ref[...]).astype(BF)

        for n in range(3):
            qkv[r, :, n * 256 : (n + 1) * 256] = dot(normed[...], wqkv[:, n * 256 : (n + 1) * 256]).astype(BF)
        for k in range(1, n_ctx):
            j = lax.rem(ctx + k, n_ctx)
            remote(
                qkv.at[r, row_share(j), :], recv.at[ctx, r], send_sem.at[k - 1], recv_sem.at[k - 1], {"ctx": j}
            ).start()

    own_block = pltpu.make_async_copy(qkv.at[:, row_share(ctx), :], recv.at[ctx], own_sem.at[1])
    own_block.start()

    causal = lax.broadcasted_iota(jnp.int32, (cols, cols), 1) <= lax.broadcasted_iota(jnp.int32, (cols, cols), 0)

    @pl.loop(0, rows)
    def _(r):
        for h in range(2):
            q = qkv[r, :, h * HD : (h + 1) * HD]
            key = qkv[r, :, 256 + h * HD : 256 + (h + 1) * HD]
            val = qkv[r, :, 512 + h * HD : 512 + (h + 1) * HD]
            scores = jnp.where(causal, dot_t(q, key) * HD ** (-0.5), NEG)
            top = jnp.max(scores, axis=-1, keepdims=True)
            weights = jnp.where(causal, jnp.exp(scores - top), 0.0)
            acc[r, :, h * HD : (h + 1) * HD] = dot(weights.astype(BF), val)
            maxes[r, :, h * HD : (h + 1) * HD] = jnp.broadcast_to(top, (cols, HD))
            sums[r, :, h * HD : (h + 1) * HD] = jnp.broadcast_to(jnp.sum(weights, axis=-1, keepdims=True), (cols, HD))

    own_block.wait()
    for k in range(1, n_ctx):
        source = lax.rem(ctx + n_ctx - k, n_ctx)
        remote(
            recv.at[source], recv.at[source], send_sem.at[k - 1], recv_sem.at[k - 1], {"ctx": source}
        ).wait_recv()

    q_id = lax.broadcasted_iota(jnp.int32, (64, 256), 0)
    k_id = lax.broadcasted_iota(jnp.int32, (64, 256), 1)
    entry = k_id // 64
    same = lax.rem(q_id, 16) == lax.rem(k_id, 16)
    earlier = same & (entry == 0) & (lax.rem(k_id, 64) // 16 < q_id // 16)
    lane = lax.broadcasted_iota(jnp.int32, (64, HD), 1)

    @pl.loop(0, n_ctx)
    def _(i):
        ids = [lists[i, l] for l in range(4)]
        fresh = []
        for l in range(1, 4):
            new = jnp.int32(1)
            for before in range(l):
                new = new * (ids[l] != ids[before]).astype(jnp.int32)
            fresh.append(new)
        usable = jnp.where(entry == 1, fresh[0], jnp.where(entry == 2, fresh[1], fresh[2]))
        mask = earlier | (same & (entry > 0) & (usable > 0))
        stats = jnp.zeros((64, HD), F32)
        for h in range(2):
            q = recv[i, :, :, h * HD : (h + 1) * HD].reshape(64, HD)
            key = jnp.concatenate(
                [recv[b, :, :, 256 + h * HD : 256 + (h + 1) * HD].reshape(64, HD) for b in ids], axis=0
            )
            val = jnp.concatenate(
                [recv[b, :, :, 512 + h * HD : 512 + (h + 1) * HD].reshape(64, HD) for b in ids], axis=0
            )
            scores = jnp.where(mask, dot_t(q, key) * HD ** (-0.5), NEG)
            top = jnp.max(scores, axis=-1, keepdims=True)
            weights = jnp.where(mask, jnp.exp(scores - top), 0.0)
            total = jnp.sum(weights, axis=-1, keepdims=True)
            part = dot(weights.astype(BF), val) / jnp.maximum(total, 1.0)
            colout[i, :, :, h * HD : (h + 1) * HD] = part.astype(BF).reshape(4, 16, HD)
            top_hi = top.astype(BF).astype(F32)
            top_mid = (top - top_hi).astype(BF).astype(F32)
            top_lo = top - top_hi - top_mid
            total_hi = total.astype(BF).astype(F32)
            pieces = [top_hi, top_mid, top_lo, total_hi, total - total_hi]
            for n, piece in enumerate(pieces):
                stats = jnp.where(lane == 8 * h + n, piece, stats)
        colout[i, :, :, 256:384] = stats.astype(BF).reshape(4, 16, HD)

    own_back = pltpu.make_async_copy(colout.at[ctx], ret.at[ctx], own_sem.at[1])
    own_back.start()
    for k in range(1, n_ctx):
        j = lax.rem(ctx + k, n_ctx)
        remote(colout.at[j], ret.at[ctx], back_send.at[k - 1], back_recv.at[k - 1], {"ctx": j}).start()

    forwards = []
    for k in range(1, 8):
        source = lax.rem(tp + 8 - k, 8)
        gather[k - 1].wait_recv()
        place = wfull_ref.at[half(source, core), :]
        forwards.append(remote(place, place, wc_send.at[k - 1], wc_recv.at[k - 1], {"ctx": sibling}))
        forwards[-1].start()

    own_back.wait()
    for k in range(1, n_ctx):
        source = lax.rem(ctx + n_ctx - k, n_ctx)
        remote(
            ret.at[source], ret.at[source], back_send.at[k - 1], back_recv.at[k - 1], {"ctx": source}
        ).wait_recv()

    @pl.loop(0, rows)
    def _(r):
        stats = ret[:, r, :, 256:384].reshape(cols, HD).astype(F32)
        for h in range(2):
            lanes = slice(h * HD, (h + 1) * HD)
            col_top = stats[:, 8 * h : 8 * h + 1] + stats[:, 8 * h + 1 : 8 * h + 2] + stats[:, 8 * h + 2 : 8 * h + 3]
            col_sum = stats[:, 8 * h + 3 : 8 * h + 4] + stats[:, 8 * h + 4 : 8 * h + 5]
            row_top = maxes[r, :, lanes]
            top = jnp.maximum(row_top, col_top)
            row_scale = jnp.exp(row_top - top)
            col_scale = jnp.exp(col_top - top) * col_sum
            part = ret[:, r, :, lanes].reshape(cols, HD).astype(F32)
            merged = (acc[r, :, lanes] * row_scale + part * col_scale) / (sums[r, :, lanes] * row_scale + col_scale)
            att_ref[pl.ds(pl.multiple_of(r * cols, cols), cols), lanes] = merged.astype(BF)

    for k in range(1, n_ctx):
        source = lax.rem(ctx + n_ctx - k, n_ctx)
        remote(
            recv.at[source], recv.at[source], send_sem.at[k - 1], recv_sem.at[k - 1], {"ctx": source}
        ).wait_send()
        remote(
            ret.at[source], ret.at[source], back_send.at[k - 1], back_recv.at[k - 1], {"ctx": source}
        ).wait_send()
    for k in range(7):
        gather[k].wait_send()
        forwards[k].wait()
    own_w.wait()


def mlp_kernel(
    att_ref, tok_ref, wout_ref, gain_ref, wup_ref, wdown_ref, out_ref,
    att, tok, wo, wu, wd, res, normed, act, terms, share, came,
    load_sem, ag_send, ag_recv, rs_send, rs_recv,
):
    chunks, chunk = 4, 256
    tp = lax.axis_index("tp")

    barrier = pltpu.get_barrier_semaphore()
    for k in range(1, 8):
        pl.semaphore_signal(barrier, inc=1, device_id={"tp": lax.rem(tp + k, 8)}, device_id_type=MESH)
    pl.semaphore_wait(barrier, 7)

    def feats(d):
        return pl.ds(pl.multiple_of(d * 256, 256), 256)

    def rows_of(c):
        return pl.ds(pl.multiple_of(c * chunk, chunk), chunk)

    def gather(c, k):
        return remote(
            att_ref.at[rows_of(c), :], att.at[rows_of(c), feats(tp)],
            ag_send.at[c, k - 1], ag_recv.at[c, k - 1], {"tp": lax.rem(tp + k, 8)},
        )

    def scatter(c, k):
        d = lax.rem(tp + k, 8)
        return remote(
            terms.at[rows_of(c), feats(d)], came.at[k - 1, rows_of(c), :],
            rs_send.at[c, k - 1], rs_recv.at[c, k - 1], {"tp": d},
        )

    @pl.loop(0, chunks)
    def _(c):
        for k in range(1, 8):
            gather(c, k).start()

    loads = [
        pltpu.make_async_copy(att_ref, att.at[:, feats(tp)], load_sem.at[0]),
        pltpu.make_async_copy(wout_ref, wo, load_sem.at[1]),
        pltpu.make_async_copy(tok_ref, tok, load_sem.at[2]),
        pltpu.make_async_copy(wup_ref, wu, load_sem.at[3]),
        pltpu.make_async_copy(wdown_ref, wd, load_sem.at[4]),
    ]
    for load in loads:
        load.start()
    for load in loads:
        load.wait()

    @pl.loop(0, chunks)
    def _(c):
        rows = rows_of(c)
        for k in range(1, 8):
            gather(c, k).wait_recv()

        @pl.loop(0, 8)
        def _(n):
            res[:, feats(n)] = tok[rows, feats(n)].astype(F32) + dot(att[rows, :], wo[:, feats(n)])

        @pl.loop(0, chunk // 64)
        def _(b):
            part = pl.ds(pl.multiple_of(b * 64, 64), 64)
            normed[part, :] = layer_norm(res[part, :], gain_ref[...]).astype(BF)

        share[rows, :] = res[:, feats(tp)]

        @pl.loop(0, 4)
        def _(n):
            act[:, feats(n)] = jax.nn.gelu(dot(normed[...], wu[:, feats(n)])).astype(BF)

        for k in range(1, 9):
            d = lax.rem(tp + k, 8)
            terms[rows, feats(d)] = dot(act[...], wd[:, feats(d)]).astype(BF)
            if k < 8:
                scatter(c, k).start()

    @pl.loop(0, chunks)
    def _(c):
        rows = rows_of(c)
        total = share[rows, :] + terms[rows, feats(tp)].astype(F32)
        for k in range(1, 8):
            scatter(c, k).wait_recv()
            total = total + came[k - 1, rows, :].astype(F32)
        out_ref[rows, :] = total.astype(BF)

    @pl.loop(0, chunks)
    def _(c):
        for k in range(1, 8):
            gather(c, k).wait_send()
            scatter(c, k).wait_send()


ANY = pl.BlockSpec(memory_space=pl.ANY)
VMEM = pl.BlockSpec(memory_space=pltpu.VMEM)
SMEM = pl.BlockSpec(memory_space=pltpu.SMEM)
DMA = pltpu.SemaphoreType.DMA


def on_device(tokens, block_lists, gain_attn, w_qkv, w_out, gain_mlp, w_up, w_down):
    rows, cols, width = tokens.shape
    flat = tokens.reshape(rows * cols, width)
    attended, w_full = pl.pallas_call(
        attn_kernel,
        out_shape=(
            jax.ShapeDtypeStruct((rows * cols, 256), BF),
            jax.ShapeDtypeStruct((width, width), BF),
        ),
        in_specs=[SMEM, ANY, VMEM, ANY, ANY],
        out_specs=(VMEM, ANY),
        scratch_shapes=[
            pltpu.VMEM((4, 256, 2048), BF),
            pltpu.VMEM((2048, 768), BF),
            pltpu.VMEM((256, 2048), BF),
            pltpu.VMEM((4, 256, 768), BF),
            pltpu.VMEM((16, 4, 16, 768), BF),
            pltpu.VMEM((16, 4, 16, 384), BF),
            pltpu.VMEM((16, 4, 16, 384), BF),
            pltpu.VMEM((4, 256, 256), F32),
            pltpu.VMEM((4, 256, 256), F32),
            pltpu.VMEM((4, 256, 256), F32),
            DMA((5,)), DMA((2,)), DMA((15,)), DMA((15,)), DMA((15,)), DMA((15,)),
            DMA((7,)), DMA((7,)), DMA((7,)), DMA((7,)),
        ],
        compiler_params=pltpu.CompilerParams(collective_id=0, has_side_effects=True, vmem_limit_bytes=56 << 20),
        name="attn",
    )(block_lists, flat, gain_attn.reshape(1, width), w_qkv.reshape(width, 768), w_out)
    out = pl.pallas_call(
        mlp_kernel,
        out_shape=jax.ShapeDtypeStruct((rows * cols, 256), BF),
        in_specs=[ANY, ANY, ANY, VMEM, ANY, ANY],
        out_specs=VMEM,
        scratch_shapes=[
            pltpu.VMEM((1024, 2048), BF),
            pltpu.VMEM((1024, 2048), BF),
            pltpu.VMEM((2048, 2048), BF),
            pltpu.VMEM((2048, 1024), BF),
            pltpu.VMEM((1024, 2048), BF),
            pltpu.VMEM((256, 2048), F32),
            pltpu.VMEM((256, 2048), BF),
            pltpu.VMEM((256, 1024), BF),
            pltpu.VMEM((1024, 2048), BF),
            pltpu.VMEM((1024, 256), F32),
            pltpu.VMEM((7, 1024, 256), BF),
            DMA((5,)), DMA((4, 7)), DMA((4, 7)), DMA((4, 7)), DMA((4, 7)),
        ],
        compiler_params=pltpu.CompilerParams(collective_id=1, has_side_effects=True, vmem_limit_bytes=56 << 20),
        name="mlp",
    )(attended, flat, w_full, gain_mlp.reshape(1, width), w_up, w_down)
    return out.reshape(rows, cols, 256)


def solution(mesh):
    return jax.shard_map(
        on_device,
        mesh=mesh,
        in_specs=(
            P("ctx", None, None),
            P(),
            P(),
            P(None, None, "tp"),
            P("tp", None),
            P(),
            P(None, "tp"),
            P("tp", None),
        ),
        out_specs=P("ctx", None, "tp"),
        check_vma=False,
    )
```

time: 472 us -> 207 us (0.44)
  waiting for transfers between devices: 354 us -> 0 us
  Pallas kernels: 0 us -> 195 us
  matrix products: 58.6 us -> 0 us
  other arithmetic: 22.6 us -> 0 us
  local copies, waits for them, and re-layouts: 22.8 us -> 9.28 us
  between operations: 13.3 us -> 0.03 us
    pallas_call x0 -> x2, Pallas kernels: none -> 195 us  [the longest x1 98.9 us: on_device(): pl.pallas_call(mlp_kernel, out_shape=jax.ShapeDtypeStruct((rows * cols, 2...]
    psum x1 -> x0, waiting for transfers between devices: 186 us -> none  [on_device(): summed = lax.psum(head_terms.astype(jnp.bfloat16), 'tp').astype(jnp.float32)]
    all_gather x2 -> x0, waiting for transfers between devices: 84.8 us -> none  [the longest x1 47.8 us: on_device(): key_piece = lax.all_gather(key_heads, 'ctx', axis=0, tiled=True)]
    reduce_scatter x1 -> x0, waiting for transfers between devices: 83.7 us -> none  [on_device(): lax.psum_scatter(down_terms.astype(jnp.bfloat16), 'tp', scatter_dimension...]
    dot_general x7 -> x0, matrix products: 58.6 us -> none  [the longest x1 16.2 us: on_device(): down_terms = jnp.dot(activated, w_down, preferred_element_type=jnp.float32)]
    reduce_sum x6 -> x0, other arithmetic: 16.9 us -> none  [the longest x2 7.71 us: layer_norm(): centre = jnp.mean(values, axis=-1, keepdims=True)]
    convert_element_type x2 -> x0, other arithmetic: 5.46 us -> none  [the longest x1 3.16 us: on_device(): normed = layer_norm(flat_tokens, gain_attn).astype(jnp.bfloat16)]
    unnamed x26 -> x3, local copies, waits for them, and re-layouts: 10.1 us -> 6.42 us
  transfers between devices with their start and end apart: 4 -> 0, of which waited for: 4 -> 0; matrix products, arithmetic and copies ran while one was open for 5% -> 0% of each run, Pallas kernels for 0% -> 0%
where the time goes in v1:
time: 207 us; the launch traced here: 205 us
  Pallas kernels  195 us (94%)
  local copies, waits for them, and re-layouts  9.28 us (4%)
    pallas_call x1, Pallas kernels, on_device(): pl.pallas_call(mlp_kernel, out_shape=jax.ShapeDtypeStruct((rows * cols, 2...  98.9 us
    pallas_call x1, Pallas kernels, on_device(): pl.pallas_call(attn_kernel, out_shape=(jax.ShapeDtypeStruct((rows * cols,...  96.4 us
    unnamed x3, local copies, waits for them, and re-layouts  6.42 us

profile of v1, /device:TPU:0, one launch (start us, length us, event | category | flops | bytes accessed | tf_op | source)
XLA Modules:
  0.0 204.6 jit_solution(14022650332972598755)
XLA Ops:
  0.0 1.4 copy.12.lists
  1.4 3.2 %copy.11 = bf16[2048,3,256]{0,2,1:T(8,128)(2,1)S(1)} copy(bf16[2048,3,256]{2,0,1:T(8,128)(2,1)} %param.11) | data formatting | bytes 6291456 | tf_op args[3]
  4.6 2.9 %copy.13.wqkv_ref = bf16[2048,768]{1,0:T(8,128)(2,1)} copy(bf16[2048,768]{0,1:T(8,128)(2,1)S(1)} %bitcast.7) | data formatting | bytes 6291456 | tf_op jit(solution)/shard_map/reshape | solution.py:345
  7.4 96.4 %attn.1 = (bf16[1024,256]{1,0:T(8,128)(2,1)}, bf16[2048,2048]{1,0:T(8,128)(2,1)}) custom-call(s32[16,4]{1,0:T(8,128)} %copy.12.lists, bf16[1024,2048]{1,0:T(8,128)(2,1)} %bitcast.5, f32[1,2048]{1,0:T(1,128)} %bitcast.10, bf16[2048,768]{1,0:T(8,128)(2,1)} %copy.13.wqkv_ref, bf16[256,2048]{1,0:T(8,128)(2,1)} %wout_ref.1), custom_call_target="tpu_custom_call" | custom-call | tf_op jit(solution)/shard_map/attn/pallas_call | solution.py:321
  103.8 98.9 %mlp.1 = bf16[1024,256]{1,0:T(8,128)(2,1)} custom-call(bf16[1024,256]{1,0:T(8,128)(2,1)} %get-tuple-element.7.att_ref, bf16[1024,2048]{1,0:T(8,128)(2,1)} %bitcast.6, bf16[2048,2048]{1,0:T(8,128)(2,1)} %get-tuple-element.8.wout_ref, f32[1,2048]{1,0:T(1,128)} %bitcast.9, bf16[2048,1024]{1,0:T(8,128)(2,1)} %wup_ref.1, bf16[1024,2048]{1,0:T(8,128)(2,1)} %wdown_ref.1), custom_call_target="tpu_custom_call" | custom-call | tf_op jit(solution)/shard_map/mlp/pallas_call | solution.py:346
  202.8 1.9 copy.15

commit v2 on v1

--- a/solution.py
+++ b/solution.py
@@ -10,6 +10,8 @@
 HD = 128
 MESH = pl.DeviceIdType.MESH
 NEG = -1e30
+CHUNKS = 4
+AHEAD = 3
 BF = jnp.bfloat16
 F32 = jnp.float32
 
@@ -33,6 +35,16 @@
 
 def dot_t(a, b):
     return lax.dot_general(a, b, (((1,), (1,)), ((), ())), preferred_element_type=F32)
+
+
+class places:
+    def __init__(self, tp):
+        def other(d):
+            return d + 1 - 2 * lax.rem(d, 2)
+
+        self.x = other(tp)
+        self.up, self.down, self.far = (lax.rem(tp + step, 8) for step in (2, 6, 4))
+        self.up_x, self.down_x, self.far_x = other(self.up), other(self.down), other(self.far)
 
 
 def attn_kernel(
@@ -64,19 +76,34 @@
         pl.semaphore_signal(barrier, inc=1, device_id={"tp": lax.rem(tp + k, 8)}, device_id_type=MESH)
     pl.semaphore_wait(barrier, n_ctx - 1 + 7)
 
-    def half(owner, which):
-        return pl.ds(pl.multiple_of(owner * 256 + which * 128, 128), 128)
-
-    gather = []
-    for k in range(1, 8):
-        gather.append(
-            remote(
-                wout_ref.at[pl.ds(pl.multiple_of(core * 128, 128), 128), :],
-                wfull_ref.at[half(tp, core), :],
-                wo_send.at[k - 1], wo_recv.at[k - 1], {"tp": lax.rem(tp + k, 8)},
-            )
-        )
-        gather[-1].start()
+    here = places(tp)
+
+    def w_rows(owner, begin=0, size=128):
+        return wfull_ref.at[pl.ds(pl.multiple_of(owner * 256 + core * 128 + begin, 64), size), :]
+
+    def pass_on(kind, owner, device, begin=0, size=128):
+        place = w_rows(owner, begin, size)
+        return remote(place, place, wo_send.at[kind], wo_recv.at[kind], {"tp": device})
+
+    own_half = wout_ref.at[pl.ds(pl.multiple_of(core * 128, 128), 128), :]
+    w_first = [
+        remote(own_half, w_rows(tp), wo_send.at[kind], wo_recv.at[kind], {"tp": device})
+        for kind, device in enumerate((here.x, here.up, here.down))
+    ]
+    w_across = [pass_on(3, here.x, here.up), pass_on(4, here.x, here.down)]
+    w_halves = [pass_on(5, here.down, here.up, 0, 64), pass_on(6, here.up, here.down, 64, 64)]
+    w_last = [pass_on(7, here.down_x, here.up, 0, 64), pass_on(8, here.up_x, here.down, 64, 64)]
+
+    def to_sibling(kind, owner):
+        place = w_rows(owner)
+        return remote(place, place, wc_send.at[kind], wc_recv.at[kind], {"ctx": sibling})
+
+    siblings = [
+        to_sibling(kind, owner)
+        for kind, owner in enumerate((here.x, here.up, here.down, here.up_x, here.down_x, here.far, here.far_x))
+    ]
+    for copy in w_first:
+        copy.start()
 
     loads[0].wait()
 
@@ -87,13 +114,11 @@
     def _(r):
         pltpu.make_async_copy(tok_ref.at[pl.ds(0, cols), :], tok.at[r], load_sem.at[r]).wait()
 
-        @pl.loop(0, cols // 64)
-        def _(b):
-            part = pl.ds(pl.multiple_of(b * 64, 64), 64)
+        for b in range(cols // 64):
+            part = slice(b * 64, (b + 1) * 64)
             normed[part, :] = layer_norm(tok[r, part, :].astype(F32), gain_ref[...]).astype(BF)
-
         for n in range(3):
-            qkv[r, :, n * 256 : (n + 1) * 256] = dot(normed[...], wqkv[:, n * 256 : (n + 1) * 256]).astype(BF)
+            qkv[r, :, n * 256 : (n + 1) * 256] = dot(normed[...], wqkv[n]).astype(BF)
         for k in range(1, n_ctx):
             j = lax.rem(ctx + k, n_ctx)
             remote(
@@ -118,6 +143,11 @@
             maxes[r, :, h * HD : (h + 1) * HD] = jnp.broadcast_to(top, (cols, HD))
             sums[r, :, h * HD : (h + 1) * HD] = jnp.broadcast_to(jnp.sum(weights, axis=-1, keepdims=True), (cols, HD))
 
+    for copy in w_first:
+        copy.wait_recv()
+    for copy in w_across + w_halves + siblings[:3]:
+        copy.start()
+
     own_block.wait()
     for k in range(1, n_ctx):
         source = lax.rem(ctx + n_ctx - k, n_ctx)
@@ -132,9 +162,8 @@
     earlier = same & (entry == 0) & (lax.rem(k_id, 64) // 16 < q_id // 16)
     lane = lax.broadcasted_iota(jnp.int32, (64, HD), 1)
 
-    @pl.loop(0, n_ctx)
-    def _(i):
-        ids = [lists[i, l] for l in range(4)]
+    def column_block(i):
+        ids = [lists[l, i] for l in range(4)]
         fresh = []
         for l in range(1, 4):
             new = jnp.int32(1)
@@ -167,19 +196,24 @@
                 stats = jnp.where(lane == 8 * h + n, piece, stats)
         colout[i, :, :, 256:384] = stats.astype(BF).reshape(4, 16, HD)
 
+    @pl.loop(0, n_ctx // 4)
+    def _(group):
+        for member in range(4):
+            column_block(group * 4 + member)
+
     own_back = pltpu.make_async_copy(colout.at[ctx], ret.at[ctx], own_sem.at[1])
     own_back.start()
     for k in range(1, n_ctx):
         j = lax.rem(ctx + k, n_ctx)
         remote(colout.at[j], ret.at[ctx], back_send.at[k - 1], back_recv.at[k - 1], {"ctx": j}).start()
 
-    forwards = []
-    for k in range(1, 8):
-        source = lax.rem(tp + 8 - k, 8)
-        gather[k - 1].wait_recv()
-        place = wfull_ref.at[half(source, core), :]
-        forwards.append(remote(place, place, wc_send.at[k - 1], wc_recv.at[k - 1], {"ctx": sibling}))
-        forwards[-1].start()
+    for copy in w_across:
+        copy.wait_recv()
+    for copy in w_last + siblings[3:5]:
+        copy.start()
+    for copy in w_halves:
+        copy.wait_recv()
+    siblings[5].start()
 
     own_back.wait()
     for k in range(1, n_ctx):
@@ -211,9 +245,13 @@
         remote(
             ret.at[source], ret.at[source], back_send.at[k - 1], back_recv.at[k - 1], {"ctx": source}
         ).wait_send()
-    for k in range(7):
-        gather[k].wait_send()
-        forwards[k].wait()
+    for copy in w_last:
+        copy.wait_recv()
+    siblings[6].start()
+    for copy in w_first + w_across + w_halves + w_last:
+        copy.wait_send()
+    for copy in siblings:
+        copy.wait()
     own_w.wait()
 
 
@@ -222,13 +260,15 @@
     att, tok, wo, wu, wd, res, normed, act, terms, share, came,
     load_sem, ag_send, ag_recv, rs_send, rs_recv,
 ):
-    chunks, chunk = 4, 256
+    chunks, chunk = CHUNKS, 1024 // CHUNKS
+    half = chunk // 2
     tp = lax.axis_index("tp")
+    here = places(tp)
 
     barrier = pltpu.get_barrier_semaphore()
-    for k in range(1, 8):
-        pl.semaphore_signal(barrier, inc=1, device_id={"tp": lax.rem(tp + k, 8)}, device_id_type=MESH)
-    pl.semaphore_wait(barrier, 7)
+    for d in (here.x, here.up, here.down):
+        pl.semaphore_signal(barrier, inc=1, device_id={"tp": d}, device_id_type=MESH)
+    pl.semaphore_wait(barrier, 3)
 
     def feats(d):
         return pl.ds(pl.multiple_of(d * 256, 256), 256)
@@ -236,24 +276,123 @@
     def rows_of(c):
         return pl.ds(pl.multiple_of(c * chunk, chunk), chunk)
 
-    def gather(c, k):
+    def low(c):
+        return pl.ds(pl.multiple_of(c * chunk, half), half)
+
+    def high(c):
+        return pl.ds(pl.multiple_of(c * chunk + half, half), half)
+
+    def gather(kind, c, rows, owner, device):
+        place = att.at[rows, feats(owner)]
+        source = att_ref.at[rows, :] if kind < 3 else place
+        return remote(source, place, ag_send.at[kind, c], ag_recv.at[kind, c], {"tp": device})
+
+    gathers = (
+        lambda c: gather(0, c, rows_of(c), tp, here.x),
+        lambda c: gather(1, c, rows_of(c), tp, here.up),
+        lambda c: gather(2, c, rows_of(c), tp, here.down),
+        lambda c: gather(3, c, rows_of(c), here.x, here.up),
+        lambda c: gather(4, c, rows_of(c), here.x, here.down),
+        lambda c: gather(5, c, low(c), here.down, here.up),
+        lambda c: gather(6, c, high(c), here.up, here.down),
+        lambda c: gather(7, c, rows_of(c), here.far, here.x),
+    )
+
+    def scatter(kind, c, rows, owner, device, slot):
         return remote(
-            att_ref.at[rows_of(c), :], att.at[rows_of(c), feats(tp)],
-            ag_send.at[c, k - 1], ag_recv.at[c, k - 1], {"tp": lax.rem(tp + k, 8)},
+            terms.at[rows, feats(owner)], came.at[slot, rows, :],
+            rs_send.at[kind, c], rs_recv.at[kind, c], {"tp": device},
         )
 
-    def scatter(c, k):
-        d = lax.rem(tp + k, 8)
-        return remote(
-            terms.at[rows_of(c), feats(d)], came.at[k - 1, rows_of(c), :],
-            rs_send.at[c, k - 1], rs_recv.at[c, k - 1], {"tp": d},
-        )
-
-    @pl.loop(0, chunks)
-    def _(c):
-        for k in range(1, 8):
-            gather(c, k).start()
-
+    scatters = (
+        lambda c: scatter(0, c, rows_of(c), here.far_x, here.x, 0),
+        lambda c: scatter(1, c, rows_of(c), here.up_x, here.up, 1),
+        lambda c: scatter(2, c, rows_of(c), here.down_x, here.down, 2),
+        lambda c: scatter(3, c, low(c), here.far, here.up, 3),
+        lambda c: scatter(4, c, high(c), here.far, here.down, 3),
+        lambda c: scatter(5, c, rows_of(c), here.up, here.up, 4),
+        lambda c: scatter(6, c, rows_of(c), here.down, here.down, 5),
+        lambda c: scatter(7, c, rows_of(c), here.x, here.x, 6),
+    )
+
+    def start(copies, kinds, c):
+        for kind in kinds:
+            copies[kind](c).start()
+
+    def arrive(copies, kinds, c):
+        for kind in kinds:
+            copies[kind](c).wait_recv()
+
+    def add(rows, owner, slots):
+        total = terms[rows, feats(owner)].astype(F32)
+        for slot in slots:
+            total = total + came[slot, rows, :].astype(F32)
+        return total
+
+    def when(c, step):
+        @pl.when((c >= 0) & (c < chunks))
+        def _():
+            step(c)
+
+    def ag_begin(c):
+        start(gathers, (0, 1, 2), c)
+
+    def ag_across(c):
+        arrive(gathers, (0, 1, 2), c)
+        start(gathers, (3, 4, 5, 6), c)
+
+    def ag_far(c):
+        arrive(gathers, (5, 6), c)
+        start(gathers, (7,), c)
+
+    def ag_end(c):
+        arrive(gathers, (3, 4, 7), c)
+
+    def rs_far(c):
+        arrive(scatters, (0,), c)
+        terms[rows_of(c), feats(here.far)] = add(rows_of(c), here.far, [0]).astype(BF)
+        start(scatters, (3, 4), c)
+
+    def rs_across(c):
+        arrive(scatters, (1, 2), c)
+        terms[rows_of(c), feats(here.x)] = add(rows_of(c), here.x, [1, 2]).astype(BF)
+        start(scatters, (7,), c)
+
+    def rs_near(c):
+        arrive(scatters, (3,), c)
+        terms[low(c), feats(here.up)] = add(low(c), here.up, [3]).astype(BF)
+        start(scatters, (5,), c)
+        arrive(scatters, (4,), c)
+        terms[high(c), feats(here.down)] = add(high(c), here.down, [3]).astype(BF)
+        start(scatters, (6,), c)
+
+    def rs_end(c):
+        arrive(scatters, (5, 6, 7), c)
+        rows = rows_of(c)
+        out_ref[rows, :] = (share[rows, :] + add(rows, tp, [4, 5, 6])).astype(BF)
+
+    def compute_up(c):
+        rows = rows_of(c)
+        for n in range(8):
+            cols = slice(n * 256, (n + 1) * 256)
+            res[:, cols] = tok[rows, cols].astype(F32) + dot(att[rows, :], wo[:, cols])
+        for b in range(chunk // 64):
+            part = slice(b * 64, (b + 1) * 64)
+            normed[part, :] = layer_norm(res[part, :], gain_ref[...]).astype(BF)
+        share[rows, :] = res[:, feats(tp)]
+        for n in range(4):
+            cols = slice(n * 256, (n + 1) * 256)
+            act[:, cols] = jax.nn.gelu(dot(normed[...], wu[:, cols])).astype(BF)
+
+    def compute_down(c):
+        rows = rows_of(c)
+        order = (here.far_x, here.up_x, here.down_x, here.far, here.x, here.up, here.down, tp)
+        for d in order:
+            terms[rows, feats(d)] = dot(act[...], wd[:, feats(d)]).astype(BF)
+        start(scatters, (0, 1, 2), c)
+
+    for c in range(AHEAD):
+        ag_begin(c)
     loads = [
         pltpu.make_async_copy(att_ref, att.at[:, feats(tp)], load_sem.at[0]),
         pltpu.make_async_copy(wout_ref, wo, load_sem.at[1]),
@@ -263,50 +402,29 @@
     ]
     for load in loads:
         load.start()
+    ag_across(0)
+    ag_across(1)
+    ag_far(0)
     for load in loads:
         load.wait()
 
+    @pl.loop(0, chunks + 3)
+    def _(c):
+        when(c, ag_end)
+        when(c, compute_up)
+        when(c + AHEAD, ag_begin)
+        when(c + 2, ag_across)
+        when(c + 1, ag_far)
+        when(c - 1, rs_far)
+        when(c - 1, rs_across)
+        when(c - 2, rs_near)
+        when(c - 3, rs_end)
+        when(c, compute_down)
+
     @pl.loop(0, chunks)
     def _(c):
-        rows = rows_of(c)
-        for k in range(1, 8):
-            gather(c, k).wait_recv()
-
-        @pl.loop(0, 8)
-        def _(n):
-            res[:, feats(n)] = tok[rows, feats(n)].astype(F32) + dot(att[rows, :], wo[:, feats(n)])
-
-        @pl.loop(0, chunk // 64)
-        def _(b):
-            part = pl.ds(pl.multiple_of(b * 64, 64), 64)
-            normed[part, :] = layer_norm(res[part, :], gain_ref[...]).astype(BF)
-
-        share[rows, :] = res[:, feats(tp)]
-
-        @pl.loop(0, 4)
-        def _(n):
-            act[:, feats(n)] = jax.nn.gelu(dot(normed[...], wu[:, feats(n)])).astype(BF)
-
-        for k in range(1, 9):
-            d = lax.rem(tp + k, 8)
-            terms[rows, feats(d)] = dot(act[...], wd[:, feats(d)]).astype(BF)
-            if k < 8:
-                scatter(c, k).start()
-
-    @pl.loop(0, chunks)
-    def _(c):
-        rows = rows_of(c)
-        total = share[rows, :] + terms[rows, feats(tp)].astype(F32)
-        for k in range(1, 8):
-            scatter(c, k).wait_recv()
-            total = total + came[k - 1, rows, :].astype(F32)
-        out_ref[rows, :] = total.astype(BF)
-
-    @pl.loop(0, chunks)
-    def _(c):
-        for k in range(1, 8):
-            gather(c, k).wait_send()
-            scatter(c, k).wait_send()
+        for copy in gathers + scatters:
+            copy(c).wait_send()
 
 
 ANY = pl.BlockSpec(memory_space=pl.ANY)
@@ -328,7 +446,7 @@
         out_specs=(VMEM, ANY),
         scratch_shapes=[
             pltpu.VMEM((4, 256, 2048), BF),
-            pltpu.VMEM((2048, 768), BF),
+            pltpu.VMEM((3, 2048, 256), BF),
             pltpu.VMEM((256, 2048), BF),
             pltpu.VMEM((4, 256, 768), BF),
             pltpu.VMEM((16, 4, 16, 768), BF),
@@ -338,11 +456,11 @@
             pltpu.VMEM((4, 256, 256), F32),
             pltpu.VMEM((4, 256, 256), F32),
             DMA((5,)), DMA((2,)), DMA((15,)), DMA((15,)), DMA((15,)), DMA((15,)),
-            DMA((7,)), DMA((7,)), DMA((7,)), DMA((7,)),
+            DMA((9,)), DMA((9,)), DMA((7,)), DMA((7,)),
         ],
         compiler_params=pltpu.CompilerParams(collective_id=0, has_side_effects=True, vmem_limit_bytes=56 << 20),
         name="attn",
-    )(block_lists, flat, gain_attn.reshape(1, width), w_qkv.reshape(width, 768), w_out)
+    )(block_lists.T, flat, gain_attn.reshape(1, width), jnp.transpose(w_qkv, (1, 0, 2)), w_out)
     out = pl.pallas_call(
         mlp_kernel,
         out_shape=jax.ShapeDtypeStruct((rows * cols, 256), BF),
@@ -354,13 +472,13 @@
             pltpu.VMEM((2048, 2048), BF),
             pltpu.VMEM((2048, 1024), BF),
             pltpu.VMEM((1024, 2048), BF),
-            pltpu.VMEM((256, 2048), F32),
-            pltpu.VMEM((256, 2048), BF),
-            pltpu.VMEM((256, 1024), BF),
+            pltpu.VMEM((1024 // CHUNKS, 2048), F32),
+            pltpu.VMEM((1024 // CHUNKS, 2048), BF),
+            pltpu.VMEM((1024 // CHUNKS, 1024), BF),
             pltpu.VMEM((1024, 2048), BF),
             pltpu.VMEM((1024, 256), F32),
             pltpu.VMEM((7, 1024, 256), BF),
-            DMA((5,)), DMA((4, 7)), DMA((4, 7)), DMA((4, 7)), DMA((4, 7)),
+            DMA((5,)), DMA((8, CHUNKS)), DMA((8, CHUNKS)), DMA((8, CHUNKS)), DMA((8, CHUNKS)),
         ],
         compiler_params=pltpu.CompilerParams(collective_id=1, has_side_effects=True, vmem_limit_bytes=56 << 20),
         name="mlp",

time: 207 us -> 140 us (0.68)
  Pallas kernels: 195 us -> 138 us
  local copies, waits for them, and re-layouts: 9.28 us -> 1.87 us
    pallas_call x1, Pallas kernels: 96.4 us -> 62.8 us  [on_device(): pl.pallas_call(attn_kernel, out_shape=(jax.ShapeDtypeStruct((rows * cols,...]
    pallas_call x1, Pallas kernels: 98.9 us -> 74.8 us  [on_device(): pl.pallas_call(mlp_kernel, out_shape=jax.ShapeDtypeStruct((rows * cols, 2...]
    unnamed x3 -> x1, local copies, waits for them, and re-layouts: 6.42 us -> 1.87 us
    reshape x1 -> x0, local copies, waits for them, and re-layouts: 2.86 us -> none  [on_device(): w_qkv.reshape(width, 768)]
where the time goes in v2:
time: 140 us; the launch traced here: 139 us
  Pallas kernels  138 us (99%)
  local copies, waits for them, and re-layouts  1.87 us (1%)
    pallas_call x1, Pallas kernels, on_device(): pl.pallas_call(mlp_kernel, out_shape=jax.ShapeDtypeStruct((rows * cols, 2...  74.8 us
    pallas_call x1, Pallas kernels, on_device(): pl.pallas_call(attn_kernel, out_shape=(jax.ShapeDtypeStruct((rows * cols,...  62.8 us

profile of v2, /device:TPU:0, one launch (start us, length us, event | category | flops | bytes accessed | tf_op | source)
XLA Modules:
  0.0 139.5 jit_solution(7566320720052922940)
XLA Ops:
  0.0 62.8 %attn.1 = (bf16[1024,256]{1,0:T(8,128)(2,1)}, bf16[2048,2048]{1,0:T(8,128)(2,1)}) custom-call(s32[4,16]{1,0:T(4,128)} %bitcast.12, bf16[1024,2048]{1,0:T(8,128)(2,1)} %bitcast.6, f32[1,2048]{1,0:T(1,128)} %bitcast.11, bf16[3,2048,256]{2,1,0:T(8,128)(2,1)} %bitcast.8, bf16[256,2048]{1,0:T(8,128)(2,1)} %wout_ref.1), custom_call_target="tpu_custom_call" | custom-call | tf_op jit(solution)/shard_map/attn/pallas_call | solution.py:439
  62.8 74.8 %mlp.1 = bf16[1024,256]{1,0:T(8,128)(2,1)} custom-call(bf16[1024,256]{1,0:T(8,128)(2,1)} %get-tuple-element.7.att_ref, bf16[1024,2048]{1,0:T(8,128)(2,1)} %bitcast.7, bf16[2048,2048]{1,0:T(8,128)(2,1)} %get-tuple-element.8.wout_ref, f32[1,2048]{1,0:T(1,128)} %bitcast.10, bf16[2048,1024]{1,0:T(8,128)(2,1)} %wup_ref.1, bf16[1024,2048]{1,0:T(8,128)(2,1)} %wdown_ref.1), custom_call_target="tpu_custom_call" | custom-call | tf_op jit(solution)/shard_map/mlp/pallas_call | solution.py:464
  137.6 1.9 %copy.10 = bf16[4,256,256]{2,1,0:T(8,128)(2,1)} copy(bf16[4,256,256]{2,1,0:T(8,128)(2,1)} %bitcast.9) | data formatting | bytes 1048576

commit v3 on v2

v3 whole, which is shorter than its diff:
```python
import functools

import jax
import jax.numpy as jnp
from jax import lax
from jax.experimental import pallas as pl
from jax.experimental.pallas import tpu as pltpu
from jax.sharding import PartitionSpec as P

HD = 128
MESH = pl.DeviceIdType.MESH
NEG = -1e30
CHUNKS = 4
AHEAD = 3
BF = jnp.bfloat16
F32 = jnp.float32


def remote(src, dst, send_sem, recv_sem, device):
    return pltpu.make_async_remote_copy(
        src_ref=src, dst_ref=dst, send_sem=send_sem, recv_sem=recv_sem, device_id=device, device_id_type=MESH
    )


def layer_norm(values, gain):
    centre = jnp.mean(values, axis=-1, keepdims=True)
    centred = values - centre
    variance = jnp.mean(centred * centred, axis=-1, keepdims=True)
    return centred * lax.rsqrt(variance + 1e-05) * gain


def dot(a, b):
    return jnp.dot(a, b, preferred_element_type=F32)


def dot_t(a, b):
    return lax.dot_general(a, b, (((1,), (1,)), ((), ())), preferred_element_type=F32)


class places:
    def __init__(self, tp):
        def other(d):
            return d + 1 - 2 * lax.rem(d, 2)

        self.x = other(tp)
        self.up, self.down, self.far = (lax.rem(tp + step, 8) for step in (2, 6, 4))
        self.up_x, self.down_x, self.far_x = other(self.up), other(self.down), other(self.far)


def layer_kernel(
    lists, tok_ref, gain_attn_ref, wqkv_ref, wout_ref, gain_mlp_ref, wup_ref, wdown_ref, out_ref,
    tok, wqkv, normed, qkv, recv_0, recv_1, colout, ret, acc, maxes, sums,
    att, wo, wu, wd, res, act, terms, share, came,
    tok_sem, load_sem, own_sem, back_sem, send_sem, recv_sem, back_send, back_recv,
    wo_send, wo_recv, wc_send, wc_recv, ag_send, ag_recv, rs_send, rs_recv,
):
    n_ctx, rows, cols = 16, 4, 256
    recv = (recv_0, recv_1)
    part_cols = cols // n_ctx
    ctx = lax.axis_index("ctx")
    tp = lax.axis_index("tp")
    here = places(tp)
    core = lax.rem(ctx, 2)
    sibling = ctx + 1 - 2 * core

    def feats(d):
        return pl.ds(pl.multiple_of(d * 256, 256), 256)

    def row_tokens(r):
        return pl.ds(pl.multiple_of(r * cols, cols), cols)

    def tok_load(r):
        return pltpu.make_async_copy(tok_ref.at[row_tokens(r), :], tok.at[row_tokens(r), :], tok_sem.at[r])

    wqkv_load = pltpu.make_async_copy(wqkv_ref, wqkv, load_sem.at[0])
    loads = [
        pltpu.make_async_copy(wout_ref, wo.at[feats(tp), :], load_sem.at[1]),
        pltpu.make_async_copy(wup_ref, wu, load_sem.at[2]),
        pltpu.make_async_copy(wdown_ref, wd, load_sem.at[3]),
    ]
    tok_load(0).start()
    wqkv_load.start()
    for r in range(1, rows):
        tok_load(r).start()

    barrier = pltpu.get_barrier_semaphore()
    for k in range(1, n_ctx):
        pl.semaphore_signal(barrier, inc=1, device_id={"ctx": lax.rem(ctx + k, n_ctx)}, device_id_type=MESH)
    for d in (here.x, here.up, here.down):
        pl.semaphore_signal(barrier, inc=1, device_id={"tp": d}, device_id_type=MESH)
    pl.semaphore_wait(barrier, n_ctx - 1 + 3)

    def w_rows(owner, begin=0, size=128):
        return wo.at[pl.ds(pl.multiple_of(owner * 256 + core * 128 + begin, 64), size), :]

    def pass_on(kind, owner, device, begin=0, size=128):
        place = w_rows(owner, begin, size)
        return remote(place, place, wo_send.at[kind], wo_recv.at[kind], {"tp": device})

    own_half = wout_ref.at[pl.ds(pl.multiple_of(core * 128, 128), 128), :]
    w_first = [
        remote(own_half, w_rows(tp), wo_send.at[kind], wo_recv.at[kind], {"tp": device})
        for kind, device in enumerate((here.x, here.up, here.down))
    ]
    w_across = [pass_on(3, here.x, here.up), pass_on(4, here.x, here.down)]
    w_halves = [pass_on(5, here.down, here.up, 0, 64), pass_on(6, here.up, here.down, 64, 64)]
    w_last = [pass_on(7, here.down_x, here.up, 0, 64), pass_on(8, here.up_x, here.down, 64, 64)]

    def to_sibling(kind, owner):
        place = w_rows(owner)
        return remote(place, place, wc_send.at[kind], wc_recv.at[kind], {"ctx": sibling})

    siblings = [
        to_sibling(kind, owner)
        for kind, owner in enumerate((here.x, here.up, here.down, here.up_x, here.down_x, here.far, here.far_x))
    ]
    for copy in w_first:
        copy.start()

    def col_share(j):
        return pl.ds(pl.multiple_of(j * part_cols, part_cols), part_cols)

    def exchange(h, k):
        source = lax.rem(ctx + n_ctx - k, n_ctx)
        place = recv[h].at[source]
        return remote(place, place, send_sem.at[h, k - 1], recv_sem.at[h, k - 1], {"ctx": source})

    def give_back(h, k):
        j = lax.rem(ctx + k, n_ctx)
        return remote(colout.at[h, j], ret.at[h, ctx], back_send.at[h, k - 1], back_recv.at[h, k - 1], {"ctx": j})

    own_blocks = [
        pltpu.make_async_copy(qkv.at[h, :, col_share(ctx), :], recv[h].at[ctx], own_sem.at[h]) for h in range(2)
    ]
    own_backs = [pltpu.make_async_copy(colout.at[h, ctx], ret.at[h, ctx], back_sem.at[h]) for h in range(2)]

    wqkv_load.wait()

    @pl.loop(0, rows)
    def _(r):
        tok_load(r).wait()
        for b in range(cols // 64):
            part = slice(b * 64, (b + 1) * 64)
            tokens = tok[pl.ds(pl.multiple_of(r * cols + b * 64, 64), 64), :]
            normed[part, :] = layer_norm(tokens.astype(F32), gain_attn_ref[...]).astype(BF)
        for n in range(3):
            both = dot(normed[...], wqkv[n]).astype(BF)
            for h in range(2):
                qkv[h, r, :, n * HD : (n + 1) * HD] = both[:, h * HD : (h + 1) * HD]
        for k in range(1, n_ctx):
            j = lax.rem(ctx + k, n_ctx)
            remote(
                qkv.at[0, r, col_share(j), :], recv[0].at[ctx, r],
                send_sem.at[0, k - 1], recv_sem.at[0, k - 1], {"ctx": j},
            ).start()

    for k in range(1, n_ctx):
        j = lax.rem(ctx + k, n_ctx)
        remote(
            qkv.at[1, :, col_share(j), :], recv[1].at[ctx], send_sem.at[1, k - 1], recv_sem.at[1, k - 1], {"ctx": j}
        ).start()
    for copy in own_blocks + loads:
        copy.start()

    causal = lax.broadcasted_iota(jnp.int32, (cols, cols), 1) <= lax.broadcasted_iota(jnp.int32, (cols, cols), 0)

    @pl.loop(0, rows)
    def _(r):
        for h in range(2):
            q, key, val = (qkv[h, r, :, n * HD : (n + 1) * HD] for n in range(3))
            scores = jnp.where(causal, dot_t(q, key) * HD ** (-0.5), NEG)
            top = jnp.max(scores, axis=-1, keepdims=True)
            weights = jnp.exp(scores - top)
            acc[r, :, h * HD : (h + 1) * HD] = dot(weights.astype(BF), val)
            maxes[r, :, h * HD : (h + 1) * HD] = jnp.broadcast_to(top, (cols, HD))
            sums[r, :, h * HD : (h + 1) * HD] = jnp.broadcast_to(jnp.sum(weights, axis=-1, keepdims=True), (cols, HD))

    q_id = lax.broadcasted_iota(jnp.int32, (64, 256), 0)
    k_id = lax.broadcasted_iota(jnp.int32, (64, 256), 1)
    entry = k_id // 64
    same = lax.rem(q_id, 16) == lax.rem(k_id, 16)
    earlier = same & (entry == 0) & (lax.rem(k_id, 64) // 16 < q_id // 16)
    lane = lax.broadcasted_iota(jnp.int32, (64, HD), 1)
    eye = (lax.broadcasted_iota(jnp.int32, (64, HD), 0) == lane).astype(BF)

    def turn(a):
        return lax.dot_general(a, eye[: a.shape[0]], (((0,), (0,)), ((), ())), preferred_element_type=F32)

    def column_block(h, i):
        ids = [lists[l, i] for l in range(4)]
        fresh = []
        for l in range(1, 4):
            new = jnp.int32(1)
            for before in range(l):
                new = new * (ids[l] != ids[before]).astype(jnp.int32)
            fresh.append(new)
        usable = jnp.where(entry == 1, fresh[0], jnp.where(entry == 2, fresh[1], fresh[2]))
        mask = earlier | (same & (entry > 0) & (usable > 0))
        q = recv[h][i, :, :, 0:HD].reshape(64, HD)
        key, val = (
            jnp.concatenate([recv[h][b, :, :, n * HD : (n + 1) * HD].reshape(64, HD) for b in ids], axis=0)
            for n in (1, 2)
        )
        scores = jnp.where(mask, dot_t(q, key) * HD ** (-0.5), NEG)
        top = jnp.max(scores, axis=-1, keepdims=True)
        weights = jnp.where(mask, jnp.exp(scores - top), 0.0)
        total = jnp.sum(weights, axis=-1, keepdims=True)
        colout[h, i, 0:64, :] = (dot(weights.astype(BF), val) / jnp.maximum(total, 1.0)).astype(BF)
        top_hi = top.astype(BF).astype(F32)
        top_mid = (top - top_hi).astype(BF).astype(F32)
        total_hi = total.astype(BF).astype(F32)
        stats = jnp.zeros((64, HD), F32)
        for n, piece in enumerate((top_hi, top_mid, top - top_hi - top_mid, total_hi, total - total_hi)):
            stats = jnp.where(lane == n, piece, stats)
        colout[h, i, 64:80, :] = turn(stats.astype(BF))[0:16, :].astype(BF)

    def column_part(h):
        own_blocks[h].wait()
        for k in range(1, n_ctx):
            exchange(h, k).wait_recv()

        @pl.loop(0, n_ctx // 4)
        def _(group):
            for member in range(4):
                column_block(h, group * 4 + member)

        own_backs[h].start()
        for k in range(1, n_ctx):
            give_back(h, k).start()

    def merge(h, j):
        lanes = slice(h * HD, (h + 1) * HD)
        stats = turn(ret[h, j, 64:80, :])[0:64, :]
        col_top = stats[:, 0:1] + stats[:, 1:2] + stats[:, 2:3]
        col_sum = stats[:, 3:4] + stats[:, 4:5]
        row_top, row_sum, row_part = (a[:, col_share(j), lanes].reshape(64, HD) for a in (maxes, sums, acc))
        top = jnp.maximum(row_top, col_top)
        row_scale = jnp.exp(row_top - top)
        col_scale = jnp.exp(col_top - top) * col_sum
        merged = row_part * row_scale + ret[h, j, 0:64, :].astype(F32) * col_scale
        merged = (merged / (row_sum * row_scale + col_scale)).astype(BF)
        place = pl.ds(pl.multiple_of(tp * 256 + h * HD, HD), HD)
        for r in range(rows):
            att[pl.ds(pl.multiple_of(r * cols + j * part_cols, part_cols), part_cols), place] = merged[
                r * part_cols : (r + 1) * part_cols
            ]

    def merge_part(h):
        own_backs[h].wait()
        for k in range(1, n_ctx):
            give_back(h, k).wait_recv()

        @pl.loop(0, n_ctx // 4)
        def _(group):
            for member in range(4):
                merge(h, group * 4 + member)

    for copy in w_first[1:]:
        copy.wait_recv()
    for copy in w_halves + siblings[1:3]:
        copy.start()
    w_first[0].wait_recv()
    for copy in w_across + siblings[:1]:
        copy.start()
    column_part(0)
    for copy in w_halves:
        copy.wait_recv()
    siblings[5].start()
    column_part(1)
    for copy in w_across:
        copy.wait_recv()
    for copy in w_last + siblings[3:5]:
        copy.start()
    merge_part(0)
    merge_part(1)

    chunks, chunk = CHUNKS, 1024 // CHUNKS
    half = chunk // 2

    def rows_of(c):
        return pl.ds(pl.multiple_of(c * chunk, chunk), chunk)

    def low(c):
        return pl.ds(pl.multiple_of(c * chunk, half), half)

    def high(c):
        return pl.ds(pl.multiple_of(c * chunk + half, half), half)

    def gather(kind, c, rows, owner, device):
        place = att.at[rows, feats(owner)]
        return remote(place, place, ag_send.at[kind, c], ag_recv.at[kind, c], {"tp": device})

    gathers = (
        lambda c: gather(0, c, rows_of(c), tp, here.x),
        lambda c: gather(1, c, rows_of(c), tp, here.up),
        lambda c: gather(2, c, rows_of(c), tp, here.down),
        lambda c: gather(3, c, rows_of(c), here.x, here.up),
        lambda c: gather(4, c, rows_of(c), here.x, here.down),
        lambda c: gather(5, c, low(c), here.down, here.up),
        lambda c: gather(6, c, high(c), here.up, here.down),
        lambda c: gather(7, c, rows_of(c), here.far, here.x),
    )

    def scatter(kind, c, rows, owner, device, slot):
        return remote(
            terms.at[rows, feats(owner)], came.at[slot, rows, :],
            rs_send.at[kind, c], rs_recv.at[kind, c], {"tp": device},
        )

    scatters = (
        lambda c: scatter(0, c, rows_of(c), here.far_x, here.x, 0),
        lambda c: scatter(1, c, rows_of(c), here.up_x, here.up, 1),
        lambda c: scatter(2, c, rows_of(c), here.down_x, here.down, 2),
        lambda c: scatter(3, c, low(c), here.far, here.up, 3),
        lambda c: scatter(4, c, high(c), here.far, here.down, 3),
        lambda c: scatter(5, c, rows_of(c), here.up, here.up, 4),
        lambda c: scatter(6, c, rows_of(c), here.down, here.down, 5),
        lambda c: scatter(7, c, rows_of(c), here.x, here.x, 6),
    )

    def start(copies, kinds, c):
        for kind in kinds:
            copies[kind](c).start()

    def arrive(copies, kinds, c):
        for kind in kinds:
            copies[kind](c).wait_recv()

    def add(rows, owner, slots):
        total = terms[rows, feats(owner)].astype(F32)
        for slot in slots:
            total = total + came[slot, rows, :].astype(F32)
        return total

    def when(c, step):
        @pl.when((c >= 0) & (c < chunks))
        def _():
            step(c)

    def ag_begin(c):
        start(gathers, (0, 1, 2), c)

    def ag_across(c):
        arrive(gathers, (0, 1, 2), c)
        start(gathers, (3, 4, 5, 6), c)

    def ag_far(c):
        arrive(gathers, (5, 6), c)
        start(gathers, (7,), c)

    def ag_end(c):
        arrive(gathers, (3, 4, 7), c)

    def rs_far(c):
        arrive(scatters, (0,), c)
        terms[rows_of(c), feats(here.far)] = add(rows_of(c), here.far, [0]).astype(BF)
        start(scatters, (3, 4), c)

    def rs_across(c):
        arrive(scatters, (1, 2), c)
        terms[rows_of(c), feats(here.x)] = add(rows_of(c), here.x, [1, 2]).astype(BF)
        start(scatters, (7,), c)

    def rs_near(c):
        arrive(scatters, (3,), c)
        terms[low(c), feats(here.up)] = add(low(c), here.up, [3]).astype(BF)
        start(scatters, (5,), c)
        arrive(scatters, (4,), c)
        terms[high(c), feats(here.down)] = add(high(c), here.down, [3]).astype(BF)
        start(scatters, (6,), c)

    def rs_end(c):
        arrive(scatters, (5, 6, 7), c)
        rows = rows_of(c)
        out_ref[rows, :] = (share[rows, :] + add(rows, tp, [4, 5, 6])).astype(BF)

    def compute_up(c):
        rows = rows_of(c)
        for n in range(8):
            cols = slice(n * 256, (n + 1) * 256)
            res[:, cols] = tok[rows, cols].astype(F32) + dot(att[rows, :], wo[:, cols])
        for b in range(chunk // 64):
            part = slice(b * 64, (b + 1) * 64)
            normed[part, :] = layer_norm(res[part, :], gain_mlp_ref[...]).astype(BF)
        share[rows, :] = res[:, feats(tp)]
        for n in range(4):
            cols = slice(n * 256, (n + 1) * 256)
            act[:, cols] = jax.nn.gelu(dot(normed[...], wu[:, cols])).astype(BF)

    def compute_down(c):
        rows = rows_of(c)
        order = (here.far_x, here.up_x, here.down_x, here.far, here.x, here.up, here.down, tp)
        for d in order:
            terms[rows, feats(d)] = dot(act[...], wd[:, feats(d)]).astype(BF)
        start(scatters, (0, 1, 2), c)

    for c in range(AHEAD):
        ag_begin(c)
    ag_across(0)
    ag_across(1)
    ag_far(0)
    for copy in w_last:
        copy.wait_recv()
    siblings[6].start()
    for copy in loads:
        copy.wait()
    for copy in siblings:
        copy.wait_recv()

    @pl.loop(0, chunks + 3)
    def _(c):
        when(c, ag_end)
        when(c, compute_up)
        when(c + AHEAD, ag_begin)
        when(c + 2, ag_across)
        when(c + 1, ag_far)
        when(c - 1, rs_far)
        when(c - 1, rs_across)
        when(c - 2, rs_near)
        when(c - 3, rs_end)
        when(c, compute_down)

    @pl.loop(0, chunks)
    def _(c):
        for copy in gathers + scatters:
            copy(c).wait_send()

    for copy in w_first + w_across + w_halves + w_last + siblings:
        copy.wait_send()
    for h in range(2):
        for k in range(1, n_ctx):
            exchange(h, k).wait_send()
            give_back(h, k).wait_send()


ANY = pl.BlockSpec(memory_space=pl.ANY)
VMEM = pl.BlockSpec(memory_space=pltpu.VMEM)
SMEM = pl.BlockSpec(memory_space=pltpu.SMEM)
DMA = pltpu.SemaphoreType.DMA


def on_device(tokens, block_lists, gain_attn, w_qkv, w_out, gain_mlp, w_up, w_down):
    rows, cols, width = tokens.shape
    flat = tokens.reshape(rows * cols, width)
    out = pl.pallas_call(
        layer_kernel,
        out_shape=jax.ShapeDtypeStruct((rows * cols, 256), BF),
        in_specs=[SMEM, ANY, VMEM, ANY, ANY, VMEM, ANY, ANY],
        out_specs=VMEM,
        scratch_shapes=[
            pltpu.VMEM((1024, 2048), BF),
            pltpu.VMEM((3, 2048, 256), BF),
            pltpu.VMEM((256, 2048), BF),
            pltpu.VMEM((2, 4, 256, 384), BF),
            pltpu.VMEM((16, 4, 16, 384), BF),
            pltpu.VMEM((16, 4, 16, 384), BF),
            pltpu.VMEM((2, 16, 80, 128), BF),
            pltpu.VMEM((2, 16, 80, 128), BF),
            pltpu.VMEM((4, 256, 256), F32),
            pltpu.VMEM((4, 256, 256), F32),
            pltpu.VMEM((4, 256, 256), F32),
            pltpu.VMEM((1024, 2048), BF),
            pltpu.VMEM((2048, 2048), BF),
            pltpu.VMEM((2048, 1024), BF),
            pltpu.VMEM((1024, 2048), BF),
            pltpu.VMEM((1024 // CHUNKS, 2048), F32),
            pltpu.VMEM((1024 // CHUNKS, 1024), BF),
            pltpu.VMEM((1024, 2048), BF),
            pltpu.VMEM((1024, 256), F32),
            pltpu.VMEM((7, 1024, 256), BF),
            DMA((4,)), DMA((4,)), DMA((2,)), DMA((2,)),
            DMA((2, 15)), DMA((2, 15)), DMA((2, 15)), DMA((2, 15)),
            DMA((9,)), DMA((9,)), DMA((7,)), DMA((7,)),
            DMA((8, CHUNKS)), DMA((8, CHUNKS)), DMA((8, CHUNKS)), DMA((8, CHUNKS)),
        ],
        compiler_params=pltpu.CompilerParams(collective_id=0, has_side_effects=True, vmem_limit_bytes=60 << 20),
        name="layer",
    )(
        block_lists.T, flat, gain_attn.reshape(1, width), jnp.transpose(w_qkv, (1, 0, 2)), w_out,
        gain_mlp.reshape(1, width), w_up, w_down,
    )
    return out.reshape(rows, cols, 256)


def solution(mesh):
    return jax.shard_map(
        on_device,
        mesh=mesh,
        in_specs=(
            P("ctx", None, None),
            P(),
            P(),
            P(None, None, "tp"),
            P("tp", None),
            P(),
            P(None, "tp"),
            P("tp", None),
        ),
        out_specs=P("ctx", None, "tp"),
        check_vma=False,
    )
```

time: 140 us -> 126 us (0.900)
  Pallas kernels: 138 us -> 124 us
    pallas_call x2 -> x1, Pallas kernels: 138 us -> 124 us  [on_device(): pl.pallas_call(layer_kernel, out_shape=jax.ShapeDtypeStruct((rows * cols,...]
where the time goes in v3:
time: 126 us
  Pallas kernels  124 us (98%)
  local copies, waits for them, and re-layouts  1.87 us (1%)
    pallas_call x1, Pallas kernels, on_device(): pl.pallas_call(layer_kernel, out_shape=jax.ShapeDtypeStruct((rows * cols,...  124 us

profile of v3, /device:TPU:0, one launch (start us, length us, event | category | flops | bytes accessed | tf_op | source)
XLA Modules:
  0.0 125.8 jit_solution(7439044940974157239)
XLA Ops:
  0.0 123.9 %layer.1 = bf16[1024,256]{1,0:T(8,128)(2,1)} custom-call(s32[4,16]{1,0:T(4,128)} %bitcast.11, bf16[1024,2048]{1,0:T(8,128)(2,1)} %bitcast.6, f32[1,2048]{1,0:T(1,128)} %bitcast.9, bf16[3,2048,256]{2,1,0:T(8,128)(2,1)} %bitcast.7, bf16[256,2048]{1,0:T(8,128)(2,1)} %wout_ref.1, f32[1,2048]{1,0:T(1,128)} %bitcast.10, bf16[2048,1024]{1,0:T(8,128)(2,1)} %wup_ref.1, ...), custom_call_target="tpu_custom_call" | custom-call | tf_op jit(solution)/shard_map/layer/pallas_call | solution.py:445
  123.9 1.9 %copy.10 = bf16[4,256,256]{2,1,0:T(8,128)(2,1)} copy(bf16[4,256,256]{2,1,0:T(8,128)(2,1)} %bitcast.8) | data formatting | bytes 1048576

commit v4 on v3

--- a/solution.py
+++ b/solution.py
@@ -83,39 +83,51 @@
     for r in range(1, rows):
         tok_load(r).start()
 
+    beside = {"ctx": ctx + 2 - 4 * lax.rem(ctx // 2, 2), "tp": here.x}
+    up, down = {"tp": here.up}, {"tp": here.down}
+
     barrier = pltpu.get_barrier_semaphore()
     for k in range(1, n_ctx):
         pl.semaphore_signal(barrier, inc=1, device_id={"ctx": lax.rem(ctx + k, n_ctx)}, device_id_type=MESH)
     for d in (here.x, here.up, here.down):
         pl.semaphore_signal(barrier, inc=1, device_id={"tp": d}, device_id_type=MESH)
-    pl.semaphore_wait(barrier, n_ctx - 1 + 3)
-
-    def w_rows(owner, begin=0, size=128):
-        return wo.at[pl.ds(pl.multiple_of(owner * 256 + core * 128 + begin, 64), size), :]
-
-    def pass_on(kind, owner, device, begin=0, size=128):
-        place = w_rows(owner, begin, size)
-        return remote(place, place, wo_send.at[kind], wo_recv.at[kind], {"tp": device})
-
-    own_half = wout_ref.at[pl.ds(pl.multiple_of(core * 128, 128), 128), :]
-    w_first = [
-        remote(own_half, w_rows(tp), wo_send.at[kind], wo_recv.at[kind], {"tp": device})
-        for kind, device in enumerate((here.x, here.up, here.down))
-    ]
-    w_across = [pass_on(3, here.x, here.up), pass_on(4, here.x, here.down)]
-    w_halves = [pass_on(5, here.down, here.up, 0, 64), pass_on(6, here.up, here.down, 64, 64)]
-    w_last = [pass_on(7, here.down_x, here.up, 0, 64), pass_on(8, here.up_x, here.down, 64, 64)]
+    pl.semaphore_signal(barrier, inc=1, device_id=beside, device_id_type=MESH)
+    pl.semaphore_wait(barrier, n_ctx - 1 + 4)
+
+    def w_rows(owner, begin=0, size=64):
+        return pl.ds(pl.multiple_of(owner * 256 + core * 128 + begin, 64), size)
+
+    def w_send(kind, owner, piece, device):
+        place = wo.at[w_rows(owner, 64 * piece), :]
+        source = wout_ref.at[pl.ds(pl.multiple_of(core * 128 + 64 * piece, 64), 64), :] if kind < 6 else place
+        return remote(source, place, wo_send.at[kind], wo_recv.at[kind], device)
+
+    w_up = [w_send(0, tp, 0, up), w_send(1, tp, 1, up)]
+    w_down = [w_send(2, tp, 1, down), w_send(3, tp, 0, down)]
+    w_beside = [w_send(4, tp, 0, beside), w_send(5, tp, 1, beside)]
+    w_onward = [w_send(6, here.down, 0, up), w_send(7, here.up, 1, down)]
+    w_across = [[w_send(8 + 2 * p, here.x, p, up), w_send(9 + 2 * p, here.x, p, down)] for p in range(2)]
+    w_far = [w_send(12, here.far, 0, beside), w_send(13, here.far, 1, beside)]
+    w_all = w_up + w_down + w_beside + w_onward + w_across[0] + w_across[1] + w_far
 
     def to_sibling(kind, owner):
-        place = w_rows(owner)
+        place = wo.at[w_rows(owner, 0, 128), :]
         return remote(place, place, wc_send.at[kind], wc_recv.at[kind], {"ctx": sibling})
 
     siblings = [
         to_sibling(kind, owner)
         for kind, owner in enumerate((here.x, here.up, here.down, here.up_x, here.down_x, here.far, here.far_x))
     ]
-    for copy in w_first:
-        copy.start()
+
+    def start_all(copies):
+        for copy in copies:
+            copy.start()
+
+    def arrive_all(copies):
+        for copy in copies:
+            copy.wait_recv()
+
+    start_all([w_up[0], w_down[0], w_beside[0], w_up[1], w_down[1], w_beside[1]])
 
     def col_share(j):
         return pl.ds(pl.multiple_of(j * part_cols, part_cols), part_cols)
@@ -161,6 +173,11 @@
         ).start()
     for copy in own_blocks + loads:
         copy.start()
+
+    arrive_all([w_up[0], w_down[0]])
+    start_all(w_onward)
+    arrive_all([w_beside[0]])
+    start_all(w_across[0])
 
     causal = lax.broadcasted_iota(jnp.int32, (cols, cols), 1) <= lax.broadcasted_iota(jnp.int32, (cols, cols), 0)
 
@@ -255,22 +272,17 @@
             for member in range(4):
                 merge(h, group * 4 + member)
 
-    for copy in w_first[1:]:
-        copy.wait_recv()
-    for copy in w_halves + siblings[1:3]:
-        copy.start()
-    w_first[0].wait_recv()
-    for copy in w_across + siblings[:1]:
-        copy.start()
+    arrive_all([w_beside[1]])
+    start_all(w_across[1])
+    arrive_all([w_up[1], w_down[1]])
+    start_all(siblings[:3])
     column_part(0)
-    for copy in w_halves:
-        copy.wait_recv()
-    siblings[5].start()
+    arrive_all(w_onward)
+    start_all(w_far)
+    start_all(siblings[5:6])
     column_part(1)
-    for copy in w_across:
-        copy.wait_recv()
-    for copy in w_last + siblings[3:5]:
-        copy.start()
+    arrive_all(w_across[0] + w_across[1])
+    start_all(siblings[3:5])
     merge_part(0)
     merge_part(1)
 
@@ -385,7 +397,7 @@
         share[rows, :] = res[:, feats(tp)]
         for n in range(4):
             cols = slice(n * 256, (n + 1) * 256)
-            act[:, cols] = jax.nn.gelu(dot(normed[...], wu[:, cols])).astype(BF)
+            act[:, cols] = jax.nn.gelu(dot(normed[0:chunk, :], wu[:, cols])).astype(BF)
 
     def compute_down(c):
         rows = rows_of(c)
@@ -399,33 +411,31 @@
     ag_across(0)
     ag_across(1)
     ag_far(0)
-    for copy in w_last:
-        copy.wait_recv()
-    siblings[6].start()
+    arrive_all(w_far)
+    start_all(siblings[6:])
     for copy in loads:
         copy.wait()
-    for copy in siblings:
-        copy.wait_recv()
+    arrive_all(siblings)
 
     @pl.loop(0, chunks + 3)
     def _(c):
         when(c, ag_end)
-        when(c, compute_up)
         when(c + AHEAD, ag_begin)
         when(c + 2, ag_across)
         when(c + 1, ag_far)
+        when(c, compute_up)
         when(c - 1, rs_far)
+        when(c, compute_down)
         when(c - 1, rs_across)
         when(c - 2, rs_near)
         when(c - 3, rs_end)
-        when(c, compute_down)
 
     @pl.loop(0, chunks)
     def _(c):
         for copy in gathers + scatters:
             copy(c).wait_send()
 
-    for copy in w_first + w_across + w_halves + w_last + siblings:
+    for copy in w_all + siblings:
         copy.wait_send()
     for h in range(2):
         for k in range(1, n_ctx):
@@ -470,7 +480,7 @@
             pltpu.VMEM((7, 1024, 256), BF),
             DMA((4,)), DMA((4,)), DMA((2,)), DMA((2,)),
             DMA((2, 15)), DMA((2, 15)), DMA((2, 15)), DMA((2, 15)),
-            DMA((9,)), DMA((9,)), DMA((7,)), DMA((7,)),
+            DMA((14,)), DMA((14,)), DMA((7,)), DMA((7,)),
             DMA((8, CHUNKS)), DMA((8, CHUNKS)), DMA((8, CHUNKS)), DMA((8, CHUNKS)),
         ],
         compiler_params=pltpu.CompilerParams(collective_id=0, has_side_effects=True, vmem_limit_bytes=60 << 20),

time: 126 us -> 111 us (0.88)
  Pallas kernels: 124 us -> 109 us
    pallas_call x1, Pallas kernels: 124 us -> 109 us  [on_device(): pl.pallas_call(layer_kernel, out_shape=jax.ShapeDtypeStruct((rows * cols,...]
where the time goes in v4:
time: 111 us
  Pallas kernels  109 us (98%)
  local copies, waits for them, and re-layouts  1.87 us (2%)
    pallas_call x1, Pallas kernels, on_device(): pl.pallas_call(layer_kernel, out_shape=jax.ShapeDtypeStruct((rows * cols,...  109 us

profile of v4, /device:TPU:0, one launch (start us, length us, event | category | flops | bytes accessed | tf_op | source)
XLA Modules:
  0.0 110.7 jit_solution(17423535947736129964)
XLA Ops:
  0.0 108.8 %layer.1 = bf16[1024,256]{1,0:T(8,128)(2,1)} custom-call(s32[4,16]{1,0:T(4,128)} %bitcast.11, bf16[1024,2048]{1,0:T(8,128)(2,1)} %bitcast.6, f32[1,2048]{1,0:T(1,128)} %bitcast.9, bf16[3,2048,256]{2,1,0:T(8,128)(2,1)} %bitcast.7, bf16[256,2048]{1,0:T(8,128)(2,1)} %wout_ref.1, f32[1,2048]{1,0:T(1,128)} %bitcast.10, bf16[2048,1024]{1,0:T(8,128)(2,1)} %wup_ref.1, ...), custom_call_target="tpu_custom_call" | custom-call | tf_op jit(solution)/shard_map/layer/pallas_call | solution.py:455
  108.8 1.9 %copy.10 = bf16[4,256,256]{2,1,0:T(8,128)(2,1)} copy(bf16[4,256,256]{2,1,0:T(8,128)(2,1)} %bitcast.8) | data formatting | bytes 1048576

commit v5 on v4

--- a/solution.py
+++ b/solution.py
@@ -69,6 +69,9 @@
     def row_tokens(r):
         return pl.ds(pl.multiple_of(r * cols, cols), cols)
 
+    def head_lanes(h):
+        return pl.ds(pl.multiple_of(tp * 256 + h * HD, HD), HD)
+
     def tok_load(r):
         return pltpu.make_async_copy(tok_ref.at[row_tokens(r), :], tok.at[row_tokens(r), :], tok_sem.at[r])
 
@@ -92,6 +95,15 @@
     for d in (here.x, here.up, here.down):
         pl.semaphore_signal(barrier, inc=1, device_id={"tp": d}, device_id_type=MESH)
     pl.semaphore_signal(barrier, inc=1, device_id=beside, device_id_type=MESH)
+
+    def norm(r):
+        for b in range(cols // 64):
+            part = slice(b * 64, (b + 1) * 64)
+            tokens = tok[pl.ds(pl.multiple_of(r * cols + b * 64, 64), 64), :]
+            normed[lax.rem(r, 2), part, :] = layer_norm(tokens.astype(F32), gain_attn_ref[...]).astype(BF)
+
+    tok_load(0).wait()
+    norm(0)
     pl.semaphore_wait(barrier, n_ctx - 1 + 4)
 
     def w_rows(owner, begin=0, size=64):
@@ -106,9 +118,10 @@
     w_down = [w_send(2, tp, 1, down), w_send(3, tp, 0, down)]
     w_beside = [w_send(4, tp, 0, beside), w_send(5, tp, 1, beside)]
     w_onward = [w_send(6, here.down, 0, up), w_send(7, here.up, 1, down)]
-    w_across = [[w_send(8 + 2 * p, here.x, p, up), w_send(9 + 2 * p, here.x, p, down)] for p in range(2)]
+    w_across = [w_send(8, here.x, 0, down), w_send(9, here.x, 1, up)]
+    w_near = [w_send(10, here.down, 0, beside), w_send(11, here.up, 1, beside)]
     w_far = [w_send(12, here.far, 0, beside), w_send(13, here.far, 1, beside)]
-    w_all = w_up + w_down + w_beside + w_onward + w_across[0] + w_across[1] + w_far
+    w_all = w_up + w_down + w_beside + w_onward + w_across + w_near + w_far
 
     def to_sibling(kind, owner):
         place = wo.at[w_rows(owner, 0, 128), :]
@@ -139,7 +152,7 @@
 
     def give_back(h, k):
         j = lax.rem(ctx + k, n_ctx)
-        return remote(colout.at[h, j], ret.at[h, ctx], back_send.at[h, k - 1], back_recv.at[h, k - 1], {"ctx": j})
+        return remote(colout.at[h, j], ret.at[h, ctx], back_send.at[h, k], back_recv.at[h, k], {"ctx": j})
 
     own_blocks = [
         pltpu.make_async_copy(qkv.at[h, :, col_share(ctx), :], recv[h].at[ctx], own_sem.at[h]) for h in range(2)
@@ -147,16 +160,14 @@
     own_backs = [pltpu.make_async_copy(colout.at[h, ctx], ret.at[h, ctx], back_sem.at[h]) for h in range(2)]
 
     wqkv_load.wait()
+    for r in range(1, rows):
+        tok_load(r).wait()
 
     @pl.loop(0, rows)
     def _(r):
-        tok_load(r).wait()
-        for b in range(cols // 64):
-            part = slice(b * 64, (b + 1) * 64)
-            tokens = tok[pl.ds(pl.multiple_of(r * cols + b * 64, 64), 64), :]
-            normed[part, :] = layer_norm(tokens.astype(F32), gain_attn_ref[...]).astype(BF)
+        norm(jnp.minimum(r + 1, rows - 1))
         for n in range(3):
-            both = dot(normed[...], wqkv[n]).astype(BF)
+            both = dot(normed[lax.rem(r, 2)], wqkv[n]).astype(BF)
             for h in range(2):
                 qkv[h, r, :, n * HD : (n + 1) * HD] = both[:, h * HD : (h + 1) * HD]
         for k in range(1, n_ctx):
@@ -175,9 +186,9 @@
         copy.start()
 
     arrive_all([w_up[0], w_down[0]])
-    start_all(w_onward)
+    start_all(w_onward + w_near)
     arrive_all([w_beside[0]])
-    start_all(w_across[0])
+    start_all(w_across[:1])
 
     causal = lax.broadcasted_iota(jnp.int32, (cols, cols), 1) <= lax.broadcasted_iota(jnp.int32, (cols, cols), 0)
 
@@ -239,11 +250,17 @@
         @pl.loop(0, n_ctx // 4)
         def _(group):
             for member in range(4):
-                column_block(h, group * 4 + member)
-
-        own_backs[h].start()
-        for k in range(1, n_ctx):
-            give_back(h, k).start()
+                column_block(h, lax.rem(ctx + group * 4 + member, n_ctx))
+            for member in range(4):
+                k = group * 4 + member
+
+                @pl.when(k == 0)
+                def _():
+                    own_backs[h].start()
+
+                @pl.when(k > 0)
+                def _():
+                    give_back(h, k).start()
 
     def merge(h, j):
         lanes = slice(h * HD, (h + 1) * HD)
@@ -256,24 +273,30 @@
         col_scale = jnp.exp(col_top - top) * col_sum
         merged = row_part * row_scale + ret[h, j, 0:64, :].astype(F32) * col_scale
         merged = (merged / (row_sum * row_scale + col_scale)).astype(BF)
-        place = pl.ds(pl.multiple_of(tp * 256 + h * HD, HD), HD)
         for r in range(rows):
-            att[pl.ds(pl.multiple_of(r * cols + j * part_cols, part_cols), part_cols), place] = merged[
+            att[pl.ds(pl.multiple_of(r * cols + j * part_cols, part_cols), part_cols), head_lanes(h)] = merged[
                 r * part_cols : (r + 1) * part_cols
             ]
 
     def merge_part(h):
-        own_backs[h].wait()
-        for k in range(1, n_ctx):
-            give_back(h, k).wait_recv()
-
         @pl.loop(0, n_ctx // 4)
         def _(group):
             for member in range(4):
-                merge(h, group * 4 + member)
+                k = group * 4 + member
+
+                @pl.when(k == 0)
+                def _():
+                    own_backs[h].wait()
+
+                @pl.when(k > 0)
+                def _():
+                    give_back(h, k).wait_recv()
+
+            for member in range(4):
+                merge(h, lax.rem(ctx + n_ctx - group * 4 - member, n_ctx))
 
     arrive_all([w_beside[1]])
-    start_all(w_across[1])
+    start_all(w_across[1:])
     arrive_all([w_up[1], w_down[1]])
     start_all(siblings[:3])
     column_part(0)
@@ -281,11 +304,8 @@
     start_all(w_far)
     start_all(siblings[5:6])
     column_part(1)
-    arrive_all(w_across[0] + w_across[1])
+    arrive_all(w_across + w_near)
     start_all(siblings[3:5])
-    merge_part(0)
-    merge_part(1)
-
     chunks, chunk = CHUNKS, 1024 // CHUNKS
     half = chunk // 2
 
@@ -298,19 +318,21 @@
     def high(c):
         return pl.ds(pl.multiple_of(c * chunk + half, half), half)
 
-    def gather(kind, c, rows, owner, device):
-        place = att.at[rows, feats(owner)]
+    def gather(kind, c, rows, owner, device, lanes=None):
+        place = att.at[rows, feats(owner) if lanes is None else lanes]
         return remote(place, place, ag_send.at[kind, c], ag_recv.at[kind, c], {"tp": device})
 
     gathers = (
         lambda c: gather(0, c, rows_of(c), tp, here.x),
-        lambda c: gather(1, c, rows_of(c), tp, here.up),
-        lambda c: gather(2, c, rows_of(c), tp, here.down),
+        lambda c: gather(1, c, rows_of(c), tp, here.up, head_lanes(0)),
+        lambda c: gather(2, c, rows_of(c), tp, here.down, head_lanes(0)),
         lambda c: gather(3, c, rows_of(c), here.x, here.up),
         lambda c: gather(4, c, rows_of(c), here.x, here.down),
         lambda c: gather(5, c, low(c), here.down, here.up),
         lambda c: gather(6, c, high(c), here.up, here.down),
         lambda c: gather(7, c, rows_of(c), here.far, here.x),
+        lambda c: gather(8, c, rows_of(c), tp, here.up, head_lanes(1)),
+        lambda c: gather(9, c, rows_of(c), tp, here.down, head_lanes(1)),
     )
 
     def scatter(kind, c, rows, owner, device, slot):
@@ -350,10 +372,10 @@
             step(c)
 
     def ag_begin(c):
-        start(gathers, (0, 1, 2), c)
+        start(gathers, (8, 9, 0), c)
 
     def ag_across(c):
-        arrive(gathers, (0, 1, 2), c)
+        arrive(gathers, (0, 1, 2, 8, 9), c)
         start(gathers, (3, 4, 5, 6), c)
 
     def ag_far(c):
@@ -393,11 +415,11 @@
             res[:, cols] = tok[rows, cols].astype(F32) + dot(att[rows, :], wo[:, cols])
         for b in range(chunk // 64):
             part = slice(b * 64, (b + 1) * 64)
-            normed[part, :] = layer_norm(res[part, :], gain_mlp_ref[...]).astype(BF)
+            normed[0, part, :] = layer_norm(res[part, :], gain_mlp_ref[...]).astype(BF)
         share[rows, :] = res[:, feats(tp)]
         for n in range(4):
             cols = slice(n * 256, (n + 1) * 256)
-            act[:, cols] = jax.nn.gelu(dot(normed[0:chunk, :], wu[:, cols])).astype(BF)
+            act[:, cols] = jax.nn.gelu(dot(normed[0, 0:chunk, :], wu[:, cols])).astype(BF)
 
     def compute_down(c):
         rows = rows_of(c)
@@ -406,6 +428,10 @@
             terms[rows, feats(d)] = dot(act[...], wd[:, feats(d)]).astype(BF)
         start(scatters, (0, 1, 2), c)
 
+    merge_part(0)
+    for c in range(chunks):
+        start(gathers, (1, 2), c)
+    merge_part(1)
     for c in range(AHEAD):
         ag_begin(c)
     ag_across(0)
@@ -460,7 +486,7 @@
         scratch_shapes=[
             pltpu.VMEM((1024, 2048), BF),
             pltpu.VMEM((3, 2048, 256), BF),
-            pltpu.VMEM((256, 2048), BF),
+            pltpu.VMEM((2, 256, 2048), BF),
             pltpu.VMEM((2, 4, 256, 384), BF),
             pltpu.VMEM((16, 4, 16, 384), BF),
             pltpu.VMEM((16, 4, 16, 384), BF),
@@ -479,9 +505,9 @@
             pltpu.VMEM((1024, 256), F32),
             pltpu.VMEM((7, 1024, 256), BF),
             DMA((4,)), DMA((4,)), DMA((2,)), DMA((2,)),
-            DMA((2, 15)), DMA((2, 15)), DMA((2, 15)), DMA((2, 15)),
+            DMA((2, 15)), DMA((2, 15)), DMA((2, 16)), DMA((2, 16)),
             DMA((14,)), DMA((14,)), DMA((7,)), DMA((7,)),
-            DMA((8, CHUNKS)), DMA((8, CHUNKS)), DMA((8, CHUNKS)), DMA((8, CHUNKS)),
+            DMA((10, CHUNKS)), DMA((10, CHUNKS)), DMA((8, CHUNKS)), DMA((8, CHUNKS)),
         ],
         compiler_params=pltpu.CompilerParams(collective_id=0, has_side_effects=True, vmem_limit_bytes=60 << 20),
         name="layer",

time: 111 us -> 106 us (0.955)
  Pallas kernels: 109 us -> 104 us
    pallas_call x1, Pallas kernels: 109 us -> 104 us  [on_device(): pl.pallas_call(layer_kernel, out_shape=jax.ShapeDtypeStruct((rows * cols,...]
where the time goes in v5:
time: 106 us
  Pallas kernels  104 us (98%)
  local copies, waits for them, and re-layouts  1.87 us (2%)
    pallas_call x1, Pallas kernels, on_device(): pl.pallas_call(layer_kernel, out_shape=jax.ShapeDtypeStruct((rows * cols,...  104 us

profile of v5, /device:TPU:0, one launch (start us, length us, event | category | flops | bytes accessed | tf_op | source)
XLA Modules:
  0.0 105.6 jit_solution(5928729299027579917)
XLA Ops:
  0.0 103.8 %layer.1 = bf16[1024,256]{1,0:T(8,128)(2,1)} custom-call(s32[4,16]{1,0:T(4,128)} %bitcast.11, bf16[1024,2048]{1,0:T(8,128)(2,1)} %bitcast.6, f32[1,2048]{1,0:T(1,128)} %bitcast.9, bf16[3,2048,256]{2,1,0:T(8,128)(2,1)} %bitcast.7, bf16[256,2048]{1,0:T(8,128)(2,1)} %wout_ref.1, f32[1,2048]{1,0:T(1,128)} %bitcast.10, bf16[2048,1024]{1,0:T(8,128)(2,1)} %wup_ref.1, ...), custom_call_target="tpu_custom_call" | custom-call | tf_op jit(solution)/shard_map/layer/pallas_call | solution.py:481
  103.8 1.9 %copy.10 = bf16[4,256,256]{2,1,0:T(8,128)(2,1)} copy(bf16[4,256,256]{2,1,0:T(8,128)(2,1)} %bitcast.8) | data formatting | bytes 1048576

commit v6 on v5

--- a/solution.py
+++ b/solution.py
@@ -247,12 +247,12 @@
         for k in range(1, n_ctx):
             exchange(h, k).wait_recv()
 
-        @pl.loop(0, n_ctx // 4)
+        @pl.loop(0, n_ctx // 8)
         def _(group):
-            for member in range(4):
-                column_block(h, lax.rem(ctx + group * 4 + member, n_ctx))
-            for member in range(4):
-                k = group * 4 + member
+            for member in range(8):
+                column_block(h, lax.rem(ctx + group * 8 + member, n_ctx))
+            for member in range(8):
+                k = group * 8 + member
 
                 @pl.when(k == 0)
                 def _():
@@ -279,10 +279,10 @@
             ]
 
     def merge_part(h):
-        @pl.loop(0, n_ctx // 4)
+        @pl.loop(0, n_ctx // 8)
         def _(group):
-            for member in range(4):
-                k = group * 4 + member
+            for member in range(8):
+                k = group * 8 + member
 
                 @pl.when(k == 0)
                 def _():
@@ -292,8 +292,8 @@
                 def _():
                     give_back(h, k).wait_recv()
 
-            for member in range(4):
-                merge(h, lax.rem(ctx + n_ctx - group * 4 - member, n_ctx))
+            for member in range(8):
+                merge(h, lax.rem(ctx + n_ctx - group * 8 - member, n_ctx))
 
     arrive_all([w_beside[1]])
     start_all(w_across[1:])
@@ -376,7 +376,7 @@
 
     def ag_across(c):
         arrive(gathers, (0, 1, 2, 8, 9), c)
-        start(gathers, (3, 4, 5, 6), c)
+        start(gathers, (3, 5, 4, 6), c)
 
     def ag_far(c):
         arrive(gathers, (5, 6), c)
@@ -443,7 +443,7 @@
         copy.wait()
     arrive_all(siblings)
 
-    @pl.loop(0, chunks + 3)
+    @pl.loop(0, chunks)
     def _(c):
         when(c, ag_end)
         when(c + AHEAD, ag_begin)
@@ -455,6 +455,14 @@
         when(c - 1, rs_across)
         when(c - 2, rs_near)
         when(c - 3, rs_end)
+
+    rs_far(3)
+    rs_near(2)
+    rs_across(3)
+    rs_near(3)
+    rs_end(1)
+    rs_end(2)
+    rs_end(3)
 
     @pl.loop(0, chunks)
     def _(c):

time: 106 us -> 106 us (level)
  no operation moved by 1% of the time
where the time goes in v6:
time: 106 us
  Pallas kernels  104 us (98%)
  local copies, waits for them, and re-layouts  1.87 us (2%)
    pallas_call x1, Pallas kernels, on_device(): pl.pallas_call(layer_kernel, out_shape=jax.ShapeDtypeStruct((rows * cols,...  104 us

profile of v6, /device:TPU:0, one launch (start us, length us, event | category | flops | bytes accessed | tf_op | source)
XLA Modules:
  0.0 105.6 jit_solution(1544192671536676329)
XLA Ops:
  0.0 103.7 %layer.1 = bf16[1024,256]{1,0:T(8,128)(2,1)} custom-call(s32[4,16]{1,0:T(4,128)} %bitcast.11, bf16[1024,2048]{1,0:T(8,128)(2,1)} %bitcast.6, f32[1,2048]{1,0:T(1,128)} %bitcast.9, bf16[3,2048,256]{2,1,0:T(8,128)(2,1)} %bitcast.7, bf16[256,2048]{1,0:T(8,128)(2,1)} %wout_ref.1, f32[1,2048]{1,0:T(1,128)} %bitcast.10, bf16[2048,1024]{1,0:T(8,128)(2,1)} %wup_ref.1, ...), custom_call_target="tpu_custom_call" | custom-call | tf_op jit(solution)/shard_map/layer/pallas_call | solution.py:489
  103.7 1.9 %copy.10 = bf16[4,256,256]{2,1,0:T(8,128)(2,1)} copy(bf16[4,256,256]{2,1,0:T(8,128)(2,1)} %bitcast.8) | data formatting | bytes 1048576

commit v7 on v5

--- a/solution.py
+++ b/solution.py
@@ -123,14 +123,14 @@
     w_far = [w_send(12, here.far, 0, beside), w_send(13, here.far, 1, beside)]
     w_all = w_up + w_down + w_beside + w_onward + w_across + w_near + w_far
 
-    def to_sibling(kind, owner):
-        place = wo.at[w_rows(owner, 0, 128), :]
+    def to_sibling(kind, owner, begin=0, size=128):
+        place = wo.at[w_rows(owner, begin, size), :]
         return remote(place, place, wc_send.at[kind], wc_recv.at[kind], {"ctx": sibling})
 
     siblings = [
         to_sibling(kind, owner)
-        for kind, owner in enumerate((here.x, here.up, here.down, here.up_x, here.down_x, here.far, here.far_x))
-    ]
+        for kind, owner in enumerate((here.x, here.up, here.down, here.up_x, here.down_x, here.far))
+    ] + [to_sibling(6, here.far_x, 0, 64), to_sibling(7, here.far_x, 64, 64)]
 
     def start_all(copies):
         for copy in copies:
@@ -437,8 +437,9 @@
     ag_across(0)
     ag_across(1)
     ag_far(0)
-    arrive_all(w_far)
-    start_all(siblings[6:])
+    for copy, onward in zip(w_far, siblings[6:]):
+        copy.wait_recv()
+        onward.start()
     for copy in loads:
         copy.wait()
     arrive_all(siblings)
@@ -506,7 +507,7 @@
             pltpu.VMEM((7, 1024, 256), BF),
             DMA((4,)), DMA((4,)), DMA((2,)), DMA((2,)),
             DMA((2, 15)), DMA((2, 15)), DMA((2, 16)), DMA((2, 16)),
-            DMA((14,)), DMA((14,)), DMA((7,)), DMA((7,)),
+            DMA((14,)), DMA((14,)), DMA((8,)), DMA((8,)),
             DMA((10, CHUNKS)), DMA((10, CHUNKS)), DMA((8, CHUNKS)), DMA((8, CHUNKS)),
         ],
         compiler_params=pltpu.CompilerParams(collective_id=0, has_side_effects=True, vmem_limit_bytes=60 << 20),

time: 106 us -> 105 us (level)
  no operation moved by 1% of the time
where the time goes in v7:
time: 105 us
  Pallas kernels  103 us (98%)
  local copies, waits for them, and re-layouts  1.87 us (2%)
    pallas_call x1, Pallas kernels, on_device(): pl.pallas_call(layer_kernel, out_shape=jax.ShapeDtypeStruct((rows * cols,...  103 us

profile of v7, /device:TPU:0, one launch (start us, length us, event | category | flops | bytes accessed | tf_op | source)
XLA Modules:
  0.0 104.9 jit_solution(10319387812918556668)
XLA Ops:
  0.0 103.0 %layer.1 = bf16[1024,256]{1,0:T(8,128)(2,1)} custom-call(s32[4,16]{1,0:T(4,128)} %bitcast.11, bf16[1024,2048]{1,0:T(8,128)(2,1)} %bitcast.6, f32[1,2048]{1,0:T(1,128)} %bitcast.9, bf16[3,2048,256]{2,1,0:T(8,128)(2,1)} %bitcast.7, bf16[256,2048]{1,0:T(8,128)(2,1)} %wout_ref.1, f32[1,2048]{1,0:T(1,128)} %bitcast.10, bf16[2048,1024]{1,0:T(8,128)(2,1)} %wup_ref.1, ...), custom_call_target="tpu_custom_call" | custom-call | tf_op jit(solution)/shard_map/layer/pallas_call | solution.py:482
  103.0 1.9 %copy.10 = bf16[4,256,256]{2,1,0:T(8,128)(2,1)} copy(bf16[4,256,256]{2,1,0:T(8,128)(2,1)} %bitcast.8) | data formatting | bytes 1048576
